TPU v7x, 256 devices: a whole 4x4x8 slice. The times are simulated.
256 devices in a mesh: dp: 64 (over z_lo, x, y, core), tp: 4 (over z_hi).
Axes of the slice: x: 4, y: 4, z: 8 (z_hi: 4, z_lo: 2; z = z_hi * 2 + z_lo), core: 2. Of those that a mesh axis runs over, the one named last changes fastest.
Arguments:
- tokens: bfloat16 [32768, 5120], P(('dp', 'tp')), may hold values from -24 to 24
- queries: bfloat16 [32768, 4096], P('dp', 'tp'), may hold values from -6 to 6
- grad_out: bfloat16 [32768, 4096], P('dp', 'tp'), may hold values from -6 to 6
- key_value_master_weight: float32 [2, 5120, 512], P(None, 'dp', 'tp'), may hold values from -6 to 6
- key_value_first_moment: float32 [2, 5120, 512], P(None, 'dp', 'tp'), may hold values from -6 to 6
- key_value_second_moment: float32 [2, 5120, 512], P(None, 'dp', 'tp'), may hold values from 0.5 to 8
- writer: int32 [64], replicated, may hold values from 0 to 63, each once
Outputs:
- grad_x: bfloat16 [32768, 5120], P(('dp', 'tp'))
- grad_q: bfloat16 [32768, 4096], P('dp', 'tp')
- new_master: float32 [2, 5120, 512], P(None, 'dp', 'tp')
- new_first: float32 [2, 5120, 512], P(None, 'dp', 'tp')
- new_second: float32 [2, 5120, 512], P(None, 'dp', 'tp')
- saved: bfloat16 [4096, 1280], P('dp', 'tp')
Inputs may be any that keep to these rules, and one draw needn't show every extreme that they name: writer is a permutation: each of the 64 replicas writes exactly one save shard.
All inputs are finite; a program needn't handle non-finite values.
Results may differ from a plain program's by a relative error of at most 0.017.
Values may be sent and summed in bfloat16 or wider, within the bound.
No kernel may reach another device: no remote copies, remote signals or barrier semaphores. Data moves between devices by JAX's collectives and lax.ppermute only.
A program may use at most 128 MiB of HBM per device.

v0:
```python
import functools
import math

import jax
import jax.numpy as jnp
from jax import lax
from jax.experimental import pallas as pl
from jax.experimental.pallas import tpu as pltpu
from jax.sharding import Mesh, PartitionSpec as P

HEAD_SIZE = 128


norm_eps = 1e-06
rope_base = 1000000.0
beta_one = 0.9
beta_two = 0.95
adam_eps = 1e-08
learn_rate = 0.02
weight_decay = 0.1
step_count = 10.0


def rope_tables(length, head_width):
    half_width = head_width // 2
    index_float = jnp.arange(half_width, dtype=jnp.float32)
    inverse_freq = rope_base ** (-2.0 * index_float / head_width)
    positions = jnp.arange(length, dtype=jnp.float32)
    angles = positions[:, None] * inverse_freq[None, :]
    return (jnp.cos(angles), jnp.sin(angles))


BF = jnp.bfloat16
F32 = jnp.float32
HALF = HEAD_SIZE // 2
PLACES = (0, -1, 1, 2)
NT = (((1,), (1,)), ((), ()))
TT = (((0,), (0,)), ((), ()))


def dot(left, right, dims=None):
    if dims is None:
        dims = (((1,), (0,)), ((), ()))
    return lax.dot_general(left, right, dims, preferred_element_type=F32)


def params(mebibytes=48):
    return pltpu.CompilerParams(vmem_limit_bytes=mebibytes * 1024 * 1024)


def norm_scale(field):
    return lax.rsqrt(jnp.mean(field * field, axis=-1, keepdims=True) + norm_eps)


def norm_back(field, factor, cotan):
    return factor * cotan - field * (factor * factor * factor) * jnp.mean(
        cotan * field, axis=-1, keepdims=True
    )


def turn(field, cosines, sines):
    return field * cosines + pltpu.roll(field, HALF, 1) * sines


def query_kernel(q_ref, cos_ref, sin_ref, out_ref):
    field = q_ref[...].astype(F32)
    out_ref[...] = turn(field * norm_scale(field), cos_ref[...], sin_ref[...]).astype(BF)


def rotated_queries(queries, cosines, sines):
    length, width = queries.shape
    column = pl.BlockSpec((length, HEAD_SIZE), lambda h: (0, h))
    table = pl.BlockSpec((length, HEAD_SIZE), lambda h: (0, 0))
    return pl.pallas_call(
        query_kernel,
        grid=(width // HEAD_SIZE,),
        in_specs=[column, table, table],
        out_specs=column,
        out_shape=jax.ShapeDtypeStruct(queries.shape, BF),
        compiler_params=params(),
        name="query_rope",
    )(queries, cosines, sines)


def norm_kernel(in_ref, out_ref):
    field = in_ref[...].astype(F32)
    out_ref[...] = (field * norm_scale(field)).astype(BF)


def normed(tokens):
    block = pl.BlockSpec((tokens.shape[0] // 4, tokens.shape[1]), lambda i: (i, 0))
    return pl.pallas_call(
        norm_kernel,
        grid=(4,),
        in_specs=[block],
        out_specs=block,
        out_shape=jax.ShapeDtypeStruct(tokens.shape, BF),
        compiler_params=params(),
        name="norm",
    )(tokens)


def project_kernel(scale, offset_ref, order_ref, *refs):
    x_refs, (cos_ref, sin_ref), refs = refs[:4], refs[4:6], refs[6:]
    w_refs, (whole_ref, plain_ref), out_refs = refs[:-6], refs[-6:-4], refs[-4:]
    tokens, block = cos_ref.shape[0], whole_ref.shape[0] // offset_ref.shape[0]
    at = 0
    for w_ref in w_refs:
        count = w_ref.shape[0] // block

        def step(k, carry, at=at, w_ref=w_ref):
            row = pl.ds(pl.multiple_of(offset_ref[at + k], 16), block)
            whole_ref[row, :] = w_ref[pl.ds(pl.multiple_of(k * block, 16), block), :]
            return carry

        lax.fori_loop(0, count, step, 0)
        at += count
    chunk = whole_ref.shape[0] // 4
    total = 0.0
    for j in range(4):
        columns = slice(j * chunk, (j + 1) * chunk)
        field = jnp.concatenate([x_ref[:, columns] for x_ref in x_refs], axis=0)
        total = total + dot(field, whole_ref[columns])
    plain_ref[...] = total * scale
    for k in range(4):
        rows = pl.ds(pl.multiple_of(order_ref[k] * tokens, tokens), tokens)
        u = plain_ref[rows, :HEAD_SIZE]
        out_refs[k][0] = turn(u * norm_scale(u), cos_ref[...], sin_ref[...]).astype(BF)
        out_refs[k][1] = plain_ref[rows, HEAD_SIZE:].astype(BF)


def project(offsets, order, blocks, cosines, sines, pieces, scale):
    tokens, width = cosines.shape[0], pieces[0].shape[1]
    vmem = pl.BlockSpec(memory_space=pltpu.VMEM)
    smem = pl.BlockSpec(memory_space=pltpu.SMEM)
    result = pl.pallas_call(
        functools.partial(project_kernel, scale),
        in_specs=[smem, smem] + [vmem] * (6 + len(pieces)),
        out_specs=[vmem] * 6,
        out_shape=[
            jax.ShapeDtypeStruct((blocks[0].shape[1], width), BF),
            jax.ShapeDtypeStruct((4 * tokens, width), F32),
        ]
        + [jax.ShapeDtypeStruct((2, tokens, HEAD_SIZE), BF)] * 4,
        compiler_params=params(),
        name="project",
    )(offsets, order, *blocks, cosines, sines, *pieces)
    return result[0], result[1], result[2:]


def weight_grad_kernel(offset_ref, cotan_ref, *refs):
    x_refs, out_refs, whole = refs[:4], refs[4:-1], refs[-1]
    chunk = whole.shape[0] // 8
    block = whole.shape[0] // offset_ref.shape[0]
    cotan = cotan_ref[...]
    for j in range(8):
        columns = slice(j * chunk, (j + 1) * chunk)
        field = jnp.concatenate([x_ref[:, columns] for x_ref in x_refs], axis=0)
        whole[columns] = dot(field, cotan, TT).astype(BF)
    at = 0
    for out_ref in out_refs:
        count = out_ref.shape[0] // block

        def step(k, carry, at=at, out_ref=out_ref):
            row = pl.ds(pl.multiple_of(offset_ref[at + k], 16), block)
            out_ref[pl.ds(pl.multiple_of(k * block, 16), block), :] = whole[row, :]
            return carry

        lax.fori_loop(0, count, step, 0)
        at += count


def weight_grads(offsets, blocks, cotan):
    vmem = pl.BlockSpec(memory_space=pltpu.VMEM)
    rows, width = blocks[0].shape[1], cotan.shape[1]
    return pl.pallas_call(
        weight_grad_kernel,
        in_specs=[pl.BlockSpec(memory_space=pltpu.SMEM)] + [vmem] * 5,
        out_specs=[vmem] * 4,
        out_shape=[jax.ShapeDtypeStruct((rows // 4, width), BF)] * 4,
        scratch_shapes=[pltpu.VMEM((rows, width), BF)],
        compiler_params=params(),
        name="weight_grads",
    )(offsets, cotan, *blocks)


def attention_kernel(order_ref, q_ref, g_ref, *refs):
    kv_refs, dkv_refs = refs[:4], refs[4:8]
    k_ref, ds0_ref, ds1_ref, v_ref, dk_acc, dv_acc = refs[8:]
    head = pl.program_id(0)
    length = q_ref.shape[0]
    tokens = length // 4
    mid = length // 2
    scale = 1.0 / math.sqrt(HEAD_SIZE)

    @pl.when(head == 0)
    def _():
        dk_acc[...] = jnp.zeros_like(dk_acc)
        dv_acc[...] = jnp.zeros_like(dv_acc)
        for k in range(4):
            rows = pl.ds(pl.multiple_of(order_ref[k] * tokens, tokens), tokens)
            k_ref[rows, :] = kv_refs[k][0]
            v_ref[rows, :] = kv_refs[k][1]

    q, g = q_ref[...], g_ref[...]
    k0, k1 = k_ref[:mid], k_ref[mid:]
    v0, v1 = v_ref[:mid], v_ref[mid:]
    row = lax.broadcasted_iota(jnp.int32, (mid, mid), 0)
    column = lax.broadcasted_iota(jnp.int32, (mid, mid), 1)
    allowed = row <= column
    e0 = jnp.exp(dot(k0, q, NT) * scale)
    e0a = jnp.where(allowed, e0[:, :mid], 0.0)
    e0b = e0[:, mid:]
    e1 = jnp.where(allowed, jnp.exp(dot(k1, q[mid:], NT) * scale), 0.0)
    inv_a = 1.0 / jnp.sum(e0a, axis=0, keepdims=True)
    inv_b = 1.0 / (jnp.sum(e0b, axis=0, keepdims=True) + jnp.sum(e1, axis=0, keepdims=True))
    p0a, p0b, p1 = e0a * inv_a, e0b * inv_b, e1 * inv_b
    g_a, g_b = g[:mid], g[mid:]
    dv_acc[:mid] += dot(p0a.astype(BF), g_a) + dot(p0b.astype(BF), g_b)
    dv_acc[mid:] += dot(p1.astype(BF), g_b)
    d0a, d0b, d1 = dot(v0, g_a, NT), dot(v0, g_b, NT), dot(v1, g_b, NT)
    sum_a = jnp.sum(p0a * d0a, axis=0, keepdims=True)
    sum_b = jnp.sum(p0b * d0b, axis=0, keepdims=True) + jnp.sum(p1 * d1, axis=0, keepdims=True)
    s0a = (p0a * (d0a - sum_a)).astype(BF)
    s0b = (p0b * (d0b - sum_b)).astype(BF)
    s1 = (p1 * (d1 - sum_b)).astype(BF)
    ds0_ref[0, :, :mid] = s0a
    ds0_ref[0, :, mid:] = s0b
    ds1_ref[0] = s1
    dk_acc[:mid] += dot(s0a, q[:mid]) + dot(s0b, q[mid:])
    dk_acc[mid:] += dot(s1, q[mid:])

    @pl.when(head == pl.num_programs(0) - 1)
    def _():
        for k in range(4):
            rows = pl.ds(pl.multiple_of(order_ref[k] * tokens, tokens), tokens)
            dkv_refs[k][0] = (dk_acc[rows, :] * scale).astype(BF)
            dkv_refs[k][1] = dv_acc[rows, :].astype(BF)


def attention(order, rotated, incoming, pieces):
    length, width = rotated.shape
    heads, mid = width // HEAD_SIZE, length // 2
    column = pl.BlockSpec((length, HEAD_SIZE), lambda h: (0, h))
    whole = pl.BlockSpec((length, HEAD_SIZE), lambda h: (0, 0))
    piece = pl.BlockSpec(pieces[0].shape, lambda h: (0, 0, 0))
    result = pl.pallas_call(
        attention_kernel,
        grid=(heads,),
        in_specs=[pl.BlockSpec(memory_space=pltpu.SMEM), column, column] + [piece] * 4,
        out_specs=[piece] * 4
        + [
            whole,
            pl.BlockSpec((1, mid, length), lambda h: (h, 0, 0)),
            pl.BlockSpec((1, mid, mid), lambda h: (h, 0, 0)),
        ],
        out_shape=[jax.ShapeDtypeStruct(pieces[0].shape, BF)] * 4
        + [
            jax.ShapeDtypeStruct((length, HEAD_SIZE), BF),
            jax.ShapeDtypeStruct((heads, mid, length), BF),
            jax.ShapeDtypeStruct((heads, mid, mid), BF),
        ],
        scratch_shapes=[pltpu.VMEM((length, HEAD_SIZE), BF)]
        + [pltpu.VMEM((length, HEAD_SIZE), F32)] * 2,
        compiler_params=params(60),
        name="attention",
    )(order, rotated, incoming, *pieces)
    return result[:4], result[4], result[5], result[6]


def grad_query_kernel(q_ref, k_ref, ds0_ref, ds1_ref, cos_ref, sin_ref, out_ref):
    mid = ds0_ref.shape[1]
    scale = 1.0 / math.sqrt(HEAD_SIZE)
    k0, k1 = k_ref[:mid], k_ref[mid:]
    both = dot(k0, ds0_ref[0], TT)
    early = both[:, :mid]
    late = both[:, mid:] + dot(k1, ds1_ref[0], TT)
    cotan = jnp.concatenate([early.T, late.T], axis=0) * scale
    field = q_ref[...].astype(F32)
    cotan = turn(cotan, cos_ref[...], -sin_ref[...])
    out_ref[...] = norm_back(field, norm_scale(field), cotan).astype(BF)


def grad_queries(queries, key, ds0, ds1, cosines, sines):
    length, width = queries.shape
    heads, mid = width // HEAD_SIZE, length // 2
    column = pl.BlockSpec((length, HEAD_SIZE), lambda h: (0, h))
    whole = pl.BlockSpec((length, HEAD_SIZE), lambda h: (0, 0))
    return pl.pallas_call(
        grad_query_kernel,
        grid=(heads,),
        in_specs=[
            column,
            whole,
            pl.BlockSpec((1, mid, length), lambda h: (h, 0, 0)),
            pl.BlockSpec((1, mid, mid), lambda h: (h, 0, 0)),
            whole,
            whole,
        ],
        out_specs=column,
        out_shape=jax.ShapeDtypeStruct(queries.shape, BF),
        compiler_params=params(60),
        name="grad_query",
    )(queries, key, ds0, ds1, cosines, sines)


def cotan_kernel(order_ref, b0_ref, b1_ref, b2_ref, b3_ref, plain_ref, cos_ref, sin_ref, out_ref):
    tokens = cos_ref.shape[0]
    for k, back_ref in enumerate((b0_ref, b1_ref, b2_ref, b3_ref)):
        rows = pl.ds(pl.multiple_of(order_ref[k] * tokens, tokens), tokens)
        u = plain_ref[rows, :HEAD_SIZE]
        back = turn(back_ref[0].astype(F32), cos_ref[...], -sin_ref[...])
        out_ref[rows, :HEAD_SIZE] = norm_back(u, norm_scale(u), back).astype(BF)
        out_ref[rows, HEAD_SIZE:] = back_ref[1]


def key_value_cotan(order, back, plain, cosines, sines):
    vmem = pl.BlockSpec(memory_space=pltpu.VMEM)
    return pl.pallas_call(
        cotan_kernel,
        in_specs=[pl.BlockSpec(memory_space=pltpu.SMEM)] + [vmem] * 7,
        out_specs=vmem,
        out_shape=jax.ShapeDtypeStruct(plain.shape, BF),
        compiler_params=params(),
        name="key_value_cotan",
    )(order, *back, plain, cosines, sines)


def grad_token_kernel(x_ref, kept_ref, core_ref, layer_ref, *refs):
    out_ref = refs[-1]
    cotan = kept_ref[...] + core_ref[...].astype(F32) + layer_ref[...].astype(F32)
    field = x_ref[...].astype(F32)
    out_ref[...] = norm_back(field, norm_scale(field), cotan).astype(BF)


def grad_tokens(tokens, kept, from_core, from_layer, start, given=None):
    step, width = 16, tokens.shape[1]
    first = start // step
    here = pl.BlockSpec((step, width), lambda i: (first + i, 0))
    specs = [here, here, here, pl.BlockSpec((step, width), lambda i: (i, 0))]
    operands = [tokens, kept, from_core, from_layer]
    if given is not None:
        specs.append(pl.BlockSpec(memory_space=pl.ANY))
        operands.append(given)
    return pl.pallas_call(
        grad_token_kernel,
        grid=(from_layer.shape[0] // step,),
        in_specs=specs,
        out_specs=here,
        out_shape=jax.ShapeDtypeStruct(tokens.shape, BF),
        input_output_aliases={} if given is None else {4: 0},
        compiler_params=params(),
        name="grad_tokens",
    )(*operands)


def plane_pairs(first, step):
    pairs = []
    for x in range(4):
        for y in range(4):
            for c in range(2):
                along_x = (c == 0) == first
                to_x = (x + step) % 4 if along_x else x
                to_y = y if along_x else (y + step) % 4
                pairs.append(((x * 4 + y) * 2 + c, (to_x * 4 + to_y) * 2 + c))
    return pairs


def far(block, step):
    return lax.ppermute(block, ("x", "y", "c"), plane_pairs(True, step))


def near(block, step):
    return lax.ppermute(block, ("x", "y", "c"), plane_pairs(False, step))


def swap_cores(block):
    return lax.ppermute(block, "c", [(0, 1), (1, 0)])


def group_pairs(target):
    pairs = []
    for g in range(4):
        for t in range(4):
            to_g, to_t = target(g, t)
            pairs.append((g * 4 + t, (to_g % 4) * 4 + to_t % 4))
    return pairs


def to_heads(block, k):
    return lax.ppermute(block, ("zl", "c", "t"), group_pairs(lambda g, t: (t, g + k)))


def from_heads(block, k):
    return lax.ppermute(block, ("zl", "c", "t"), group_pairs(lambda g, t: (t + k, g)))


def swap_layers(block):
    return lax.ppermute(block, "zl", [(0, 1), (1, 0)])


def after(first, *later):
    return lax.optimization_barrier((first,) + later)[1:]


def per_device(
    tokens,
    queries,
    grad_out,
    key_value_master_weight,
    key_value_first_moment,
    key_value_second_moment,
    writer,
):
    own_tokens, model_width = tokens.shape
    unit_scale = 1.0 / math.sqrt(model_width)
    length = queries.shape[0]
    rows = key_value_master_weight.shape[1]
    core = lax.axis_index("c")
    x_index, y_index = lax.axis_index("x"), lax.axis_index("y")
    t_index = lax.axis_index("t")
    g_index = 2 * lax.axis_index("zl") + core

    own_weight = key_value_master_weight.astype(BF)
    own_weight = jnp.concatenate([own_weight[0], own_weight[1]], axis=1)
    stage = jnp.concatenate([to_heads(own_weight, k) for k in range(4)], axis=0)
    own_block = normed(tokens)
    from_core = swap_cores(own_block)
    from_z = swap_layers(after(stage, own_block)[0])
    shard = jnp.concatenate([stage, near(stage, 1), near(stage, -1), near(stage, 2)], axis=0)
    pieces = [shard, far(shard, 1), far(shard, -1), far(shard, 2)]
    (from_z,) = after(pieces, from_z)
    blocks = [own_block, from_core, from_z, swap_cores(from_z)]

    place = jnp.array(PLACES, jnp.int32)
    count = jnp.arange(4, dtype=jnp.int32)
    far_place = (jnp.where(core == 0, x_index, y_index) + place) % 4
    near_place = (jnp.where(core == 0, y_index, x_index) + place) % 4
    far_step = jnp.where(core == 0, 8 * rows, 2 * rows)
    near_step = jnp.where(core == 0, 2 * rows, 8 * rows)
    source = (t_index - count) % 4
    offsets = (
        far_place[:, None, None] * far_step
        + near_place[None, :, None] * near_step
        + ((source // 2) * (32 * rows) + (source % 2) * rows)[None, None, :]
    )
    offsets = offsets.reshape(64).astype(jnp.int32)
    sequence_order = ((t_index + count) % 4) ^ g_index
    block_order = (g_index - count) % 4

    cosines, sines = rope_tables(length, HEAD_SIZE)
    cosines = jnp.concatenate([cosines, cosines], axis=1)
    sines = jnp.concatenate([-sines, sines], axis=1)
    own_cos = lax.dynamic_slice_in_dim(cosines, t_index * own_tokens, own_tokens, 0)
    own_sin = lax.dynamic_slice_in_dim(sines, t_index * own_tokens, own_tokens, 0)
    rotated = rotated_queries(queries, cosines, sines)

    weights, plain, projected = project(
        offsets, sequence_order, blocks, own_cos, own_sin,
        pieces, unit_scale,
    )
    arrived = [from_heads(block, k) for k, block in enumerate(projected)]
    returning, key, ds0, ds1 = attention(block_order, rotated, grad_out, arrived)
    back = [to_heads(block, -k) for k, block in enumerate(returning)]
    cotan = key_value_cotan(sequence_order, back, plain, own_cos, own_sin)

    part = weight_grads(offsets, blocks, cotan)
    arriving = [far(part[1], -1), far(part[2], 1), far(part[3], 2)]

    rows_of = after(part[0], cotan)[0].reshape(4, own_tokens, -1)
    sent = dot(jnp.concatenate([rows_of[1], rows_of[3]], axis=0), weights, NT) * unit_scale
    sent = sent.astype(BF)
    swapped = swap_cores(sent)
    (kept_from,) = after(sent, jnp.concatenate([rows_of[0], rows_of[2]], axis=0))
    kept = dot(kept_from, weights, NT) * unit_scale
    to_z = (kept[own_tokens:] + swapped[own_tokens:].astype(F32)).astype(BF)
    cuts = (0, 16, 64, own_tokens)
    to_z = [to_z[cuts[i] : cuts[i + 1]] for i in range(3)]
    z_first = swap_layers(to_z[0])

    own = part[0].astype(F32)
    for piece in arriving:
        own = own + piece.astype(F32)
    own = own.astype(BF).reshape(4, 4 * rows, -1)
    own, to_z[1] = after(z_first, own, to_z[1])
    z_second = swap_layers(to_z[1])
    summed = own[0].astype(F32)
    for index, step in ((1, -1), (2, 1), (3, 2)):
        summed = summed + near(own[index], step).astype(F32)

    (ds0,) = after(own, ds0)
    grad_q = grad_queries(queries, key, ds0, ds1, cosines, sines)
    (summed,) = after((grad_q, z_second), summed)

    summed = summed.astype(BF).reshape(4, rows, 2 * HEAD_SIZE)
    final = sum(from_heads(summed[k], -k).astype(F32) for k in range(4)) * unit_scale
    weight_grad = jnp.stack([final[:, :HEAD_SIZE], final[:, HEAD_SIZE:]], axis=0)

    z_first, z_second, to_z[2] = after(final, z_first, z_second, to_z[2])
    grad_x = grad_tokens(tokens, kept, swapped, z_first, 0)
    grad_x = grad_tokens(tokens, kept, swapped, z_second, cuts[1], grad_x)
    grad_x = grad_tokens(tokens, kept, swapped, swap_layers(to_z[2]), cuts[2], grad_x)

    new_first = beta_one * key_value_first_moment + (1.0 - beta_one) * weight_grad
    new_second = beta_two * key_value_second_moment + (1.0 - beta_two) * weight_grad * weight_grad
    first_hat = new_first / (1.0 - beta_one**step_count)
    second_hat = new_second / (1.0 - beta_two**step_count)
    new_master = key_value_master_weight - learn_rate * (
        first_hat / (jnp.sqrt(second_hat) + adam_eps) + weight_decay * key_value_master_weight
    )
    replicas = writer.shape[0]
    flat_saved = new_master.astype(BF).reshape(replicas, -1)
    rank_ids = jnp.arange(replicas, dtype=jnp.int32)
    inverse = jnp.sum(jnp.where(writer[None, :] == rank_ids[:, None], rank_ids[None, :], 0), axis=1)
    saved = lax.all_to_all(flat_saved[inverse], ("zl", "x", "y", "c"), 0, 0, tiled=True)
    return (grad_x, grad_q, new_master, new_first, new_second, saved)


def solution(mesh):
    fine = Mesh(mesh.devices.reshape(2, 4, 4, 2, 4), ("zl", "x", "y", "c", "t"))
    dp = ("zl", "x", "y", "c")
    every = dp + ("t",)
    weight = P(None, dp, "t")
    return jax.shard_map(
        per_device,
        mesh=fine,
        in_specs=(P(every, None), P(dp, "t"), P(dp, "t"), weight, weight, weight, P()),
        out_specs=(P(every, None), P(dp, "t"), weight, weight, weight, P(dp, "t")),
        check_vma=False,
    )
```

profile of v0, /device:TPU:1, one launch (start us, length us, event | category | flops | bytes accessed | tf_op | source)
XLA Modules:
  0.0 185.9 jit_solution(9319771503931387833)
XLA Ops:
  1.6 6.3 %collective-permute-start.1 = (bf16[80,256]{1,0:T(8,128)(2,1)S(1)}, bf16[80,256]{1,0:T(8,128)(2,1)S(1)}, u32[]{:S(2)}, u32[]{:S(2)}) collective-permute-start(bf16[80,256]{1,0:T(8,128)(2,1)S(1)} %pad_maximum_fusion.4), channel_id=1, source_target_pairs={{0,0},{1,4},{2,128},{3,132},{4,1},{5,5},{6,129},{7,133},{128,2},{1... | collective-permute-start | bytes 122888 | tf_op jit(solution)/shard_map/ppermute | solution.py:391
  7.9 4.0 %collective-permute-start.2 = (bf16[80,256]{1,0:T(8,128)(2,1)S(1)}, bf16[80,256]{1,0:T(8,128)(2,1)S(1)}, u32[]{:S(2)}, u32[]{:S(2)}) collective-permute-start(bf16[80,256]{1,0:T(8,128)(2,1)S(1)} %pad_maximum_fusion.4), channel_id=1, source_target_pairs={{0,1},{1,5},{2,129},{3,133},{4,2},{5,6},{6,130},{7,134},{128,3},{1... | collective-permute-start | bytes 122888 | tf_op jit(solution)/shard_map/ppermute | solution.py:391
  11.9 3.3 %collective-permute-start.3 = (bf16[80,256]{1,0:T(8,128)(2,1)S(1)}, bf16[80,256]{1,0:T(8,128)(2,1)S(1)}, u32[]{:S(2)}, u32[]{:S(2)}) collective-permute-start(bf16[80,256]{1,0:T(8,128)(2,1)S(1)} %pad_maximum_fusion.4), channel_id=1, source_target_pairs={{0,2},{1,6},{2,130},{3,134},{4,3},{5,7},{6,131},{7,135},{128,0},{1... | collective-permute-start | bytes 122888 | tf_op jit(solution)/shard_map/ppermute | solution.py:391
  27.4 3.0 %collective-permute-start.10 = (bf16[1280,256]{1,0:T(8,128)(2,1)S(1)}, bf16[1280,256]{1,0:T(8,128)(2,1)}, u32[]{:S(2)}, u32[]{:S(2)}) collective-permute-start(bf16[1280,256]{1,0:T(8,128)(2,1)S(1)} %constant_dynamic-update-slice_fusion.4.refs_6_), channel_id=1, source_target_pairs={{0,64},{4,20},{8,72},{12,28},{16,80},{20,4},{24,88},{28,12},{32,96... | collective-permute-start | bytes 1966088 | tf_op jit(solution)/shard_map/ppermute | solution.py:370
  33.1 6.0 %collective-permute-start = (bf16[128,5120]{1,0:T(8,128)(2,1)S(1)}, bf16[128,5120]{1,0:T(8,128)(2,1)S(1)}, u32[]{:S(2)}, u32[]{:S(2)}) collective-permute-start(bf16[128,5120]{1,0:T(8,128)(2,1)S(1)} %norm.1.refs_0_), channel_id=1, source_target_pairs={{0,4},{4,0},{1,5},{5,1},{2,6},{6,2},{3,7},{7,3},{8,12},{12,8},{9,1... | collective-permute-start | bytes 3932168 | tf_op jit(solution)/shard_map/ppermute | solution.py:378
  39.2 6.7 %collective-permute-done.8.refs_7_ = bf16[1280,256]{1,0:T(8,128)(2,1)} collective-permute-done((bf16[1280,256]{1,0:T(8,128)(2,1)S(1)}, bf16[1280,256]{1,0:T(8,128)(2,1)}, u32[]{:S(2)}, u32[]{:S(2)}) %collective-permute-start.8) | collective-permute-done | bytes 655392 | tf_op jit(solution)/shard_map/ppermute | solution.py:370
  48.4 3.6 %collective-permute-start.12 = (bf16[128,5120]{1,0:T(8,128)(2,1)}, bf16[128,5120]{1,0:T(8,128)(2,1)}, u32[]{:S(2)}, u32[]{:S(2)}) collective-permute-start(bf16[128,5120]{1,0:T(8,128)(2,1)} %collective-permute-done.11.refs_2_), channel_id=1, source_target_pairs={{0,4},{4,0},{1,5},{5,1},{2,6},{6,2},{3,7},{7,3},{8,12},{12,8},{9,1... | collective-permute-start | bytes 3932168 | tf_op jit(solution)/shard_map/ppermute | solution.py:378
  56.1 5.7 %project.1 = (bf16[5120,256]{1,0:T(8,128)(2,1)}, f32[512,256]{1,0:T(8,128)S(1)}, bf16[2,128,128]{2,1,0:T(8,128)(2,1)S(1)}, bf16[2,128,128]{2,1,0:T(8,128)(2,1)S(...) custom-call(s32[64]{0:T(128)S(1)} %add.177.offset_ref, s32[4]{0:T(128)S(1)} %fusion.19.order_ref, ...), custom_call_target="tpu_custom_call" | custom-call | tf_op jit(solution)/shard_map/project/pallas_call | solution.py:136
  66.6 4.5 %collective-permute-start.16 = (bf16[2,128,128]{2,1,0:T(8,128)(2,1)S(1)}, bf16[2,128,128]{2,1,0:T(8,128)(2,1)S(1)}, u32[]{:S(2)}, u32[]{:S(2)}) collective-permute-start(bf16[2,128,128]{2,1,0:T(8,128)(2,1)S(1)} %get-tuple-element.39), channel_id=1, source_target_pairs={{0,132},{1,0},{2,4},{3,128},{4,133},{5,1},{6,5},{7,129},{128,134},... | collective-permute-start | bytes 196616 | tf_op jit(solution)/shard_map/ppermute | solution.py:395
  72.6 4.3 %collective-permute-done.16.refs_3_ = bf16[2,128,128]{2,1,0:T(8,128)(2,1)S(1)} collective-permute-done((bf16[2,128,128]{2,1,0:T(8,128)(2,1)S(1)}, bf16[2,128,128]{2,1,0:T(8,128)(2,1)S(1)}, u32[]{:S(2)}, u32[]{:S(2)}) %collective-permute-start.16) | collective-permute-done | bytes 65568 | tf_op jit(solution)/shard_map/ppermute | solution.py:395
  77.6 10.7 %attention.1 = (bf16[2,128,128]{2,1,0:T(8,128)(2,1)}, bf16[2,128,128]{2,1,0:T(8,128)(2,1)}, bf16[2,128,128]{2,1,0:T(8,128)(2,1)}, bf16[2,128,128]{2,1,0:T(8,128)...) custom-call(s32[4]{0:T(128)} %and_select_fusion.order_ref, ...), custom_call_target="tpu_custom_call" | custom-call | tf_op jit(solution)/shard_map/attention/pallas_call | solution.py:247
  93.2 4.0 %collective-permute-start.20 = (bf16[2,128,128]{2,1,0:T(8,128)(2,1)}, bf16[2,128,128]{2,1,0:T(8,128)(2,1)S(1)}, u32[]{:S(2)}, u32[]{:S(2)}) collective-permute-start(bf16[2,128,128]{2,1,0:T(8,128)(2,1)} %get-tuple-element.43), channel_id=1, source_target_pairs={{0,1},{1,5},{2,129},{3,133},{4,2},{5,6},{6,130},{7,134},{128,3},{1... | collective-permute-start | bytes 196616 | tf_op jit(solution)/shard_map/ppermute | solution.py:391
  99.9 4.0 %weight_grads.1 = (bf16[1280,256]{1,0:T(8,128)(2,1)S(1)}, bf16[1280,256]{1,0:T(8,128)(2,1)S(1)}, bf16[1280,256]{1,0:T(8,128)(2,1)S(1)}, bf16[1280,256]{1,0:T(8,128)(2,1)S(1)}) custom-call(s32[64]{0:T(128)S(1)} %add.177.offset_ref, bf16[512,256]{1,0:T(8,128)(2,1)S(1)} %key_value_cotan.1.cotan_ref, bf16[128,5120]{1,0:T(8,128)(2,1)S(1)} %norm.1.refs_0_, ...), custom_call_target="tpu_custom_call" | custom-call | tf_op jit(solution)/shard_map/weight_grads/pallas_call | solution.py:176
  104.8 3.1 %collective-permute-start.21 = (bf16[256,5120]{1,0:T(8,128)(2,1)S(1)}, bf16[256,5120]{1,0:T(8,128)(2,1)S(1)}, u32[]{:S(2)}, u32[]{:S(2)}) collective-permute-start(bf16[256,5120]{1,0:T(8,128)(2,1)S(1)} %fusion), channel_id=1, source_target_pairs={{0,4},{4,0},{1,5},{5,1},{2,6},{6,2},{3,7},{7,3},{8,12},{12,8},{9,1... | collective-permute-start | bytes 7864328 | tf_op jit(solution)/shard_map/ppermute | solution.py:378
  115.1 3.0 %collective-permute-start.22 = (bf16[16,5120]{1,0:T(8,128)(2,1)S(1)}, bf16[16,5120]{1,0:T(8,128)(2,1)S(1)}, u32[]{:S(2)}, u32[]{:S(2)}) collective-permute-start(bf16[16,5120]{1,0:T(8,128)(2,1)S(1)} %slice.98), channel_id=1, source_target_pairs={{0,128},{128,0},{1,129},{129,1},{2,130},{130,2},{3,131},{131,3},{4... | collective-permute-start | bytes 491528 | tf_op jit(solution)/shard_map/ppermute | solution.py:399
  118.1 6.6 %collective-permute-done.23 = bf16[1280,256]{1,0:T(8,128)(2,1)S(1)} collective-permute-done((bf16[1280,256]{1,0:T(8,128)(2,1)S(1)}, bf16[1280,256]{1,0:T(8,128)(2,1)S(1)}, u32[]{:S(2)}, u32[]{:S(2)}) %collective-permute-start.23) | collective-permute-done | bytes 655392 | tf_op jit(solution)/shard_map/ppermute | solution.py:370
  124.7 3.4 %collective-permute-done.24 = bf16[1280,256]{1,0:T(8,128)(2,1)S(1)} collective-permute-done((bf16[1280,256]{1,0:T(8,128)(2,1)S(1)}, bf16[1280,256]{1,0:T(8,128)(2,1)S(1)}, u32[]{:S(2)}, u32[]{:S(2)}) %collective-permute-start.24) | collective-permute-done | bytes 655392 | tf_op jit(solution)/shard_map/ppermute | solution.py:370
  129.3 2.9 %collective-permute-start.26 = (bf16[48,5120]{1,0:T(8,128)(2,1)}, bf16[48,5120]{1,0:T(8,128)(2,1)S(1)}, u32[]{:S(2)}, u32[]{:S(2)}) collective-permute-start(bf16[48,5120]{1,0:T(8,128)(2,1)} %slice.99), channel_id=1, source_target_pairs={{0,128},{128,0},{1,129},{129,1},{2,130},{130,2},{3,131},{131,3},{4... | collective-permute-start | bytes 1474568 | tf_op jit(solution)/shard_map/ppermute | solution.py:399
  137.0 8.4 %grad_query.1 = bf16[512,1024]{1,0:T(8,128)(2,1)} custom-call(bf16[512,1024]{1,0:T(8,128)(2,1)} %q_ref.3, bf16[512,128]{1,0:T(8,128)(2,1)} %get-tuple-element.49.k_ref, bf16[8,256,512]{2,1,0:T(8,128)(2,1)} %get-tuple-element.55.ds0_ref, bf16[8,256,256]{2,1,0:T(8,128)(2,1)} %get-tuple-element.56.ds1_ref, f32[512,128]{1,0:T(8,128)} %copy-done.5, ...), custom_call_target="tpu_custom_call" | custom-call | tf_op jit(solution)/shard_map/grad_query/pallas_call | solution.py:289
  146.8 4.7 %collective-permute-start.30 = (bf16[80,256]{1,0:T(8,128)(2,1)S(1)}, bf16[80,256]{1,0:T(8,128)(2,1)S(1)}, u32[]{:S(2)}, u32[]{:S(2)}) collective-permute-start(bf16[80,256]{1,0:T(8,128)(2,1)S(1)} %get-tuple-element.73), channel_id=1, source_target_pairs={{0,0},{1,4},{2,128},{3,132},{4,1},{5,5},{6,129},{7,133},{128,2},{1... | collective-permute-start | bytes 122888 | tf_op jit(solution)/shard_map/ppermute | solution.py:395
  152.5 3.5 %collective-permute-start.32 = (bf16[80,256]{1,0:T(8,128)(2,1)S(1)}, bf16[80,256]{1,0:T(8,128)(2,1)S(1)}, u32[]{:S(2)}, u32[]{:S(2)}) collective-permute-start(bf16[80,256]{1,0:T(8,128)(2,1)S(1)} %get-tuple-element.74), channel_id=1, source_target_pairs={{0,128},{1,132},{2,0},{3,4},{4,129},{5,133},{6,1},{7,5},{128,130},... | collective-permute-start | bytes 122888 | tf_op jit(solution)/shard_map/ppermute | solution.py:395
  165.6 6.3 %all-to-all-start = ((bf16[64,2,160]{2,1,0:T(2,128)(2,1)}), bf16[64,2,160]{2,1,0:T(2,128)(2,1)S(1)}, u32[]{:S(2)}, u32[]{:S(2)}) async-start(bf16[64,2,160]{2,1,0:T(2,128)(2,1)} %reshape.152), calls=%async_computation | async-start | bytes 131072 | tf_op jit(solution)/shard_map/all_to_all | solution.py:515
  175.1 3.2 %grad_tokens.4.refs_0_ = bf16[128,5120]{1,0:T(8,128)(2,1)} custom-call(bf16[128,5120]{1,0:T(8,128)(2,1)S(1)} %copy-done.1, f32[256,5120]{1,0:T(8,128)} %copy-done.11, bf16[256,5120]{1,0:T(8,128)(2,1)S(1)} %collective-permute-done.21.core_ref, bf16[48,5120]{1,0:T(8,128)(2,1)S(1)} %copy-done.10, ...), custom_call_target="tpu_custom_call", output_to_operand_aliasing={{}: (4, {})} | custom-call | tf_op jit(solution)/shard_map/grad_tokens/pallas_call | solution.py:345
  182.1 3.8 %grad_tokens.5 = bf16[128,5120]{1,0:T(8,128)(2,1)} custom-call(bf16[128,5120]{1,0:T(8,128)(2,1)S(1)} %copy-done.2, f32[256,5120]{1,0:T(8,128)} %copy-done.11, bf16[256,5120]{1,0:T(8,128)(2,1)S(1)} %collective-permute-done.21.core_ref, bf16[64,5120]{1,0:T(8,128)(2,1)S(1)} %collective-permute-done.34.layer_ref, ...), custom_call_target="tpu_custom_call", output_to_operand_aliasing={{}: (4, {})} | custom-call | tf_op jit(solution)/shard_map/grad_tokens/pallas_call | solution.py:345
  (149 shorter events, 69.6 us)
Async XLA Ops:
  1.6 15.7 %collective-permute-start.1 = (bf16[80,256]{1,0:T(8,128)(2,1)S(1)}, bf16[80,256]{1,0:T(8,128)(2,1)S(1)}, u32[]{:S(2)}, u32[]{:S(2)}) collective-permute-start(bf16[80,256]{1,0:T(8,128)(2,1)S(1)} %pad_maximum_fusion.4), channel_id=1, source_target_pairs={{0,0},{1,4},{2,128},{3,132},{4,1},{5,5},{6,129},{7,133},{128,2},{1... | collective-permute-start | bytes 122888 | tf_op jit(solution)/shard_map/ppermute | solution.py:391
  7.9 9.4 %collective-permute-start.2 = (bf16[80,256]{1,0:T(8,128)(2,1)S(1)}, bf16[80,256]{1,0:T(8,128)(2,1)S(1)}, u32[]{:S(2)}, u32[]{:S(2)}) collective-permute-start(bf16[80,256]{1,0:T(8,128)(2,1)S(1)} %pad_maximum_fusion.4), channel_id=1, source_target_pairs={{0,1},{1,5},{2,129},{3,133},{4,2},{5,6},{6,130},{7,134},{128,3},{1... | collective-permute-start | bytes 122888 | tf_op jit(solution)/shard_map/ppermute | solution.py:391
  19.0 29.4 %collective-permute-start.11 = (bf16[128,5120]{1,0:T(8,128)(2,1)S(1)}, bf16[128,5120]{1,0:T(8,128)(2,1)}, u32[]{:S(2)}, u32[]{:S(2)}) collective-permute-start(bf16[128,5120]{1,0:T(8,128)(2,1)S(1)} %norm.1.refs_0_), channel_id=1, source_target_pairs={{0,128},{128,0},{1,129},{129,1},{2,130},{130,2},{3,131},{131,3},{4... | collective-permute-start | bytes 3932168 | tf_op jit(solution)/shard_map/ppermute | solution.py:399
  27.4 11.7 %collective-permute-start.10 = (bf16[1280,256]{1,0:T(8,128)(2,1)S(1)}, bf16[1280,256]{1,0:T(8,128)(2,1)}, u32[]{:S(2)}, u32[]{:S(2)}) collective-permute-start(bf16[1280,256]{1,0:T(8,128)(2,1)S(1)} %constant_dynamic-update-slice_fusion.4.refs_6_), channel_id=1, source_target_pairs={{0,64},{4,20},{8,72},{12,28},{16,80},{20,4},{24,88},{28,12},{32,96... | collective-permute-start | bytes 1966088 | tf_op jit(solution)/shard_map/ppermute | solution.py:370
  30.4 15.4 %collective-permute-start.8 = (bf16[1280,256]{1,0:T(8,128)(2,1)S(1)}, bf16[1280,256]{1,0:T(8,128)(2,1)}, u32[]{:S(2)}, u32[]{:S(2)}) collective-permute-start(bf16[1280,256]{1,0:T(8,128)(2,1)S(1)} %constant_dynamic-update-slice_fusion.4.refs_6_), channel_id=1, source_target_pairs={{0,32},{4,12},{8,40},{12,20},{16,48},{20,28},{24,56},{28,4},{32,64... | collective-permute-start | bytes 1966088 | tf_op jit(solution)/shard_map/ppermute | solution.py:370
  30.8 15.4 %collective-permute-start.9 = (bf16[1280,256]{1,0:T(8,128)(2,1)S(1)}, bf16[1280,256]{1,0:T(8,128)(2,1)}, u32[]{:S(2)}, u32[]{:S(2)}) collective-permute-start(bf16[1280,256]{1,0:T(8,128)(2,1)S(1)} %constant_dynamic-update-slice_fusion.4.refs_6_), channel_id=1, source_target_pairs={{0,96},{4,28},{8,104},{12,4},{16,112},{20,12},{24,120},{28,20},{32... | collective-permute-start | bytes 1966088 | tf_op jit(solution)/shard_map/ppermute | solution.py:370
  33.1 23.0 %collective-permute-start = (bf16[128,5120]{1,0:T(8,128)(2,1)S(1)}, bf16[128,5120]{1,0:T(8,128)(2,1)S(1)}, u32[]{:S(2)}, u32[]{:S(2)}) collective-permute-start(bf16[128,5120]{1,0:T(8,128)(2,1)S(1)} %norm.1.refs_0_), channel_id=1, source_target_pairs={{0,4},{4,0},{1,5},{5,1},{2,6},{6,2},{3,7},{7,3},{8,12},{12,8},{9,1... | collective-permute-start | bytes 3932168 | tf_op jit(solution)/shard_map/ppermute | solution.py:378
  48.4 7.7 %collective-permute-start.12 = (bf16[128,5120]{1,0:T(8,128)(2,1)}, bf16[128,5120]{1,0:T(8,128)(2,1)}, u32[]{:S(2)}, u32[]{:S(2)}) collective-permute-start(bf16[128,5120]{1,0:T(8,128)(2,1)} %collective-permute-done.11.refs_2_), channel_id=1, source_target_pairs={{0,4},{4,0},{1,5},{5,1},{2,6},{6,2},{3,7},{7,3},{8,12},{12,8},{9,1... | collective-permute-start | bytes 3932168 | tf_op jit(solution)/shard_map/ppermute | solution.py:378
  62.6 8.9 %collective-permute-start.13 = (bf16[2,128,128]{2,1,0:T(8,128)(2,1)S(1)}, bf16[2,128,128]{2,1,0:T(8,128)(2,1)S(1)}, u32[]{:S(2)}, u32[]{:S(2)}) collective-permute-start(bf16[2,128,128]{2,1,0:T(8,128)(2,1)S(1)} %get-tuple-element.36), channel_id=1, source_target_pairs={{0,0},{1,4},{2,128},{3,132},{4,1},{5,5},{6,129},{7,133},{128,2},{1... | collective-permute-start | bytes 196616 | tf_op jit(solution)/shard_map/ppermute | solution.py:395
  66.6 10.4 %collective-permute-start.16 = (bf16[2,128,128]{2,1,0:T(8,128)(2,1)S(1)}, bf16[2,128,128]{2,1,0:T(8,128)(2,1)S(1)}, u32[]{:S(2)}, u32[]{:S(2)}) collective-permute-start(bf16[2,128,128]{2,1,0:T(8,128)(2,1)S(1)} %get-tuple-element.39), channel_id=1, source_target_pairs={{0,132},{1,0},{2,4},{3,128},{4,133},{5,1},{6,5},{7,129},{128,134},... | collective-permute-start | bytes 196616 | tf_op jit(solution)/shard_map/ppermute | solution.py:395
  88.3 9.0 %collective-permute-start.17 = (bf16[2,128,128]{2,1,0:T(8,128)(2,1)}, bf16[2,128,128]{2,1,0:T(8,128)(2,1)S(1)}, u32[]{:S(2)}, u32[]{:S(2)}) collective-permute-start(bf16[2,128,128]{2,1,0:T(8,128)(2,1)} %get-tuple-element.40), channel_id=1, source_target_pairs={{0,0},{1,4},{2,128},{3,132},{4,1},{5,5},{6,129},{7,133},{128,2},{1... | collective-permute-start | bytes 196616 | tf_op jit(solution)/shard_map/ppermute | solution.py:391
  104.8 7.9 %collective-permute-start.21 = (bf16[256,5120]{1,0:T(8,128)(2,1)S(1)}, bf16[256,5120]{1,0:T(8,128)(2,1)S(1)}, u32[]{:S(2)}, u32[]{:S(2)}) collective-permute-start(bf16[256,5120]{1,0:T(8,128)(2,1)S(1)} %fusion), channel_id=1, source_target_pairs={{0,4},{4,0},{1,5},{5,1},{2,6},{6,2},{3,7},{7,3},{8,12},{12,8},{9,1... | collective-permute-start | bytes 7864328 | tf_op jit(solution)/shard_map/ppermute | solution.py:378
  107.9 16.8 %collective-permute-start.23 = (bf16[1280,256]{1,0:T(8,128)(2,1)S(1)}, bf16[1280,256]{1,0:T(8,128)(2,1)S(1)}, u32[]{:S(2)}, u32[]{:S(2)}) collective-permute-start(bf16[1280,256]{1,0:T(8,128)(2,1)S(1)} %get-tuple-element.50), channel_id=1, source_target_pairs={{0,96},{4,28},{8,104},{12,4},{16,112},{20,12},{24,120},{28,20},{32... | collective-permute-start | bytes 1966088 | tf_op jit(solution)/shard_map/ppermute | solution.py:370
  110.2 18.0 %collective-permute-start.24 = (bf16[1280,256]{1,0:T(8,128)(2,1)S(1)}, bf16[1280,256]{1,0:T(8,128)(2,1)S(1)}, u32[]{:S(2)}, u32[]{:S(2)}) collective-permute-start(bf16[1280,256]{1,0:T(8,128)(2,1)S(1)} %get-tuple-element.51), channel_id=1, source_target_pairs={{0,32},{4,12},{8,40},{12,20},{16,48},{20,28},{24,56},{28,4},{32,64... | collective-permute-start | bytes 1966088 | tf_op jit(solution)/shard_map/ppermute | solution.py:370
  110.2 18.0 %collective-permute-start.25 = (bf16[1280,256]{1,0:T(8,128)(2,1)S(1)}, bf16[1280,256]{1,0:T(8,128)(2,1)S(1)}, u32[]{:S(2)}, u32[]{:S(2)}) collective-permute-start(bf16[1280,256]{1,0:T(8,128)(2,1)S(1)} %get-tuple-element.52), channel_id=1, source_target_pairs={{0,64},{4,20},{8,72},{12,28},{16,80},{20,4},{24,88},{28,12},{32,96... | collective-permute-start | bytes 1966088 | tf_op jit(solution)/shard_map/ppermute | solution.py:370
  115.1 14.2 %collective-permute-start.22 = (bf16[16,5120]{1,0:T(8,128)(2,1)S(1)}, bf16[16,5120]{1,0:T(8,128)(2,1)S(1)}, u32[]{:S(2)}, u32[]{:S(2)}) collective-permute-start(bf16[16,5120]{1,0:T(8,128)(2,1)S(1)} %slice.98), channel_id=1, source_target_pairs={{0,128},{128,0},{1,129},{129,1},{2,130},{130,2},{3,131},{131,3},{4... | collective-permute-start | bytes 491528 | tf_op jit(solution)/shard_map/ppermute | solution.py:399
  129.3 17.4 %collective-permute-start.26 = (bf16[48,5120]{1,0:T(8,128)(2,1)}, bf16[48,5120]{1,0:T(8,128)(2,1)S(1)}, u32[]{:S(2)}, u32[]{:S(2)}) collective-permute-start(bf16[48,5120]{1,0:T(8,128)(2,1)} %slice.99), channel_id=1, source_target_pairs={{0,128},{128,0},{1,129},{129,1},{2,130},{130,2},{3,131},{131,3},{4... | collective-permute-start | bytes 1474568 | tf_op jit(solution)/shard_map/ppermute | solution.py:399
  133.0 12.5 %collective-permute-start.27 = (bf16[320,256]{1,0:T(8,128)(2,1)}, bf16[320,256]{1,0:T(8,128)(2,1)}, u32[]{:S(2)}, u32[]{:S(2)}) collective-permute-start(bf16[320,256]{1,0:T(8,128)(2,1)} %get-tuple-element.66), channel_id=1, source_target_pairs={{0,24},{4,100},{8,0},{12,108},{16,8},{20,116},{24,16},{28,124},{32... | collective-permute-start | bytes 491528 | tf_op jit(solution)/shard_map/ppermute | solution.py:374
  135.2 10.3 %collective-permute-start.28 = (bf16[320,256]{1,0:T(8,128)(2,1)}, bf16[320,256]{1,0:T(8,128)(2,1)}, u32[]{:S(2)}, u32[]{:S(2)}) collective-permute-start(bf16[320,256]{1,0:T(8,128)(2,1)} %get-tuple-element.68), channel_id=1, source_target_pairs={{0,8},{4,36},{8,16},{12,44},{16,24},{20,52},{24,0},{28,60},{32,40}... | collective-permute-start | bytes 491528 | tf_op jit(solution)/shard_map/ppermute | solution.py:374
  135.2 10.3 %collective-permute-start.29 = (bf16[320,256]{1,0:T(8,128)(2,1)}, bf16[320,256]{1,0:T(8,128)(2,1)}, u32[]{:S(2)}, u32[]{:S(2)}) collective-permute-start(bf16[320,256]{1,0:T(8,128)(2,1)} %get-tuple-element.67), channel_id=1, source_target_pairs={{0,16},{4,68},{8,24},{12,76},{16,0},{20,84},{24,8},{28,92},{32,48}... | collective-permute-start | bytes 491528 | tf_op jit(solution)/shard_map/ppermute | solution.py:374
  146.8 11.2 %collective-permute-start.30 = (bf16[80,256]{1,0:T(8,128)(2,1)S(1)}, bf16[80,256]{1,0:T(8,128)(2,1)S(1)}, u32[]{:S(2)}, u32[]{:S(2)}) collective-permute-start(bf16[80,256]{1,0:T(8,128)(2,1)S(1)} %get-tuple-element.73), channel_id=1, source_target_pairs={{0,0},{1,4},{2,128},{3,132},{4,1},{5,5},{6,129},{7,133},{128,2},{1... | collective-permute-start | bytes 122888 | tf_op jit(solution)/shard_map/ppermute | solution.py:395
  151.5 7.9 %collective-permute-start.31 = (bf16[80,256]{1,0:T(8,128)(2,1)S(1)}, bf16[80,256]{1,0:T(8,128)(2,1)S(1)}, u32[]{:S(2)}, u32[]{:S(2)}) collective-permute-start(bf16[80,256]{1,0:T(8,128)(2,1)S(1)} %get-tuple-element.75), channel_id=1, source_target_pairs={{0,132},{1,0},{2,4},{3,128},{4,133},{5,1},{6,5},{7,129},{128,134},... | collective-permute-start | bytes 122888 | tf_op jit(solution)/shard_map/ppermute | solution.py:395
  159.5 21.3 %collective-permute-start.34 = (bf16[64,5120]{1,0:T(8,128)(2,1)}, bf16[64,5120]{1,0:T(8,128)(2,1)S(1)}, u32[]{:S(2)}, u32[]{:S(2)}) collective-permute-start(bf16[64,5120]{1,0:T(8,128)(2,1)} %slice.104), channel_id=1, source_target_pairs={{0,128},{128,0},{1,129},{129,1},{2,130},{130,2},{3,131},{131,3},{4... | collective-permute-start | bytes 1966088 | tf_op jit(solution)/shard_map/ppermute | solution.py:399
  165.6 14.5 %all-to-all-start = ((bf16[64,2,160]{2,1,0:T(2,128)(2,1)}), bf16[64,2,160]{2,1,0:T(2,128)(2,1)S(1)}, u32[]{:S(2)}, u32[]{:S(2)}) async-start(bf16[64,2,160]{2,1,0:T(2,128)(2,1)} %reshape.152), calls=%async_computation | async-start | bytes 131072 | tf_op jit(solution)/shard_map/all_to_all | solution.py:515
  (35 other events, 311.6 us)
where the time goes:
time: 187 us; the launch traced here: 186 us
  starting transfers between devices  85.5 us (46%)
  Pallas kernels  41.8 us (22%)
  waiting for transfers between devices  35.4 us (19%)
  local copies, waits for them, and re-layouts  14.1 us (8%)
  other arithmetic  6.29 us (3%)
    ppermute x8, starting transfers between devices, to_heads(): lax.ppermute(block, ('zl', 'c', 't'), group_pairs(lambda g, t: (t, g + k)))  22.6 us
    ppermute x8, starting transfers between devices, from_heads(): lax.ppermute(block, ('zl', 'c', 't'), group_pairs(lambda g, t: (t + k, g)))  17.6 us
    ppermute x6, waiting for transfers between devices, far(): return lax.ppermute(block, ('x', 'y', 'c'), plane_pairs(True, step))  17.2 us
    ppermute x3, starting transfers between devices, swap_cores(): return lax.ppermute(block, 'c', [(0, 1), (1, 0)])  12.7 us
    pallas_call x1, Pallas kernels, attention(): pl.pallas_call(attention_kernel, grid=(heads,), in_specs=[pl.BlockSpec(me...  10.7 us
    ppermute x6, starting transfers between devices, far(): return lax.ppermute(block, ('x', 'y', 'c'), plane_pairs(True, step))  9.58 us
    unnamed x54, local copies, waits for them, and re-layouts  8.99 us
    pallas_call x3, Pallas kernels, grad_tokens(): pl.pallas_call(grad_token_kernel, grid=(from_layer.shape[0] // step,), in...  8.84 us
  transfers between devices with their start and end apart: 36, of which 14 were waited for; matrix products, arithmetic and copies ran while one was open for 7% of the time, Pallas kernels for 9%

commit v1 on v0

--- a/solution.py
+++ b/solution.py
@@ -44,7 +44,7 @@
     return lax.dot_general(left, right, dims, preferred_element_type=F32)
 
 
-def params(mebibytes=48):
+def params(mebibytes=20):
     return pltpu.CompilerParams(vmem_limit_bytes=mebibytes * 1024 * 1024)
 
 
@@ -100,28 +100,49 @@
     )(tokens)
 
 
-def project_kernel(scale, offset_ref, order_ref, *refs):
-    x_refs, (cos_ref, sin_ref), refs = refs[:4], refs[4:6], refs[6:]
-    w_refs, (whole_ref, plain_ref), out_refs = refs[:-6], refs[-6:-4], refs[-4:]
-    tokens, block = cos_ref.shape[0], whole_ref.shape[0] // offset_ref.shape[0]
+def project_early_kernel(scale, offset_ref, first_ref, second_ref, *refs):
+    w_refs, whole_ref, plain_ref = refs[:-2], refs[-2], refs[-1]
+    block = whole_ref.shape[0] // offset_ref.shape[0]
     at = 0
     for w_ref in w_refs:
         count = w_ref.shape[0] // block
-
-        def step(k, carry, at=at, w_ref=w_ref):
+        for k in range(count):
             row = pl.ds(pl.multiple_of(offset_ref[at + k], 16), block)
-            whole_ref[row, :] = w_ref[pl.ds(pl.multiple_of(k * block, 16), block), :]
-            return carry
-
-        lax.fori_loop(0, count, step, 0)
+            whole_ref[row, :] = w_ref[k * block : (k + 1) * block]
         at += count
+    plain_ref[...] = rows_times(first_ref, second_ref, whole_ref) * scale
+
+
+def rows_times(first_ref, second_ref, whole_ref):
     chunk = whole_ref.shape[0] // 4
     total = 0.0
     for j in range(4):
         columns = slice(j * chunk, (j + 1) * chunk)
-        field = jnp.concatenate([x_ref[:, columns] for x_ref in x_refs], axis=0)
+        field = jnp.concatenate([first_ref[:, columns], second_ref[:, columns]], axis=0)
         total = total + dot(field, whole_ref[columns])
-    plain_ref[...] = total * scale
+    return total
+
+
+def project_early(offsets, first, second, pieces, scale):
+    vmem = pl.BlockSpec(memory_space=pltpu.VMEM)
+    shape = (first.shape[1], pieces[0].shape[1])
+    return pl.pallas_call(
+        functools.partial(project_early_kernel, scale),
+        in_specs=[pl.BlockSpec(memory_space=pltpu.SMEM)] + [vmem] * (2 + len(pieces)),
+        out_specs=[vmem, vmem],
+        out_shape=[
+            jax.ShapeDtypeStruct(shape, BF),
+            jax.ShapeDtypeStruct((2 * first.shape[0], shape[1]), F32),
+        ],
+        compiler_params=params(48),
+        name="project_early",
+    )(offsets, first, second, *pieces)
+
+
+def project_kernel(scale, order_ref, first_ref, second_ref, whole_ref, early_ref, cos_ref, sin_ref, plain_ref, *out_refs):
+    tokens = cos_ref.shape[0]
+    plain_ref[: 2 * tokens] = early_ref[...]
+    plain_ref[2 * tokens :] = rows_times(first_ref, second_ref, whole_ref) * scale
     for k in range(4):
         rows = pl.ds(pl.multiple_of(order_ref[k] * tokens, tokens), tokens)
         u = plain_ref[rows, :HEAD_SIZE]
@@ -129,23 +150,41 @@
         out_refs[k][1] = plain_ref[rows, HEAD_SIZE:].astype(BF)
 
 
-def project(offsets, order, blocks, cosines, sines, pieces, scale):
-    tokens, width = cosines.shape[0], pieces[0].shape[1]
+def project(order, first, second, weights, early, cosines, sines, scale):
+    tokens = cosines.shape[0]
     vmem = pl.BlockSpec(memory_space=pltpu.VMEM)
-    smem = pl.BlockSpec(memory_space=pltpu.SMEM)
     result = pl.pallas_call(
         functools.partial(project_kernel, scale),
-        in_specs=[smem, smem] + [vmem] * (6 + len(pieces)),
-        out_specs=[vmem] * 6,
-        out_shape=[
-            jax.ShapeDtypeStruct((blocks[0].shape[1], width), BF),
-            jax.ShapeDtypeStruct((4 * tokens, width), F32),
-        ]
+        in_specs=[pl.BlockSpec(memory_space=pltpu.SMEM)] + [vmem] * 6,
+        out_specs=[vmem] * 5,
+        out_shape=[jax.ShapeDtypeStruct((4 * tokens, weights.shape[1]), F32)]
         + [jax.ShapeDtypeStruct((2, tokens, HEAD_SIZE), BF)] * 4,
         compiler_params=params(),
         name="project",
-    )(offsets, order, *blocks, cosines, sines, *pieces)
-    return result[0], result[1], result[2:]
+    )(order, first, second, weights, early, cosines, sines)
+    return result[0], result[1:]
+
+
+def sum_kernel(*refs):
+    in_refs, out_refs = refs[:4], refs[4:]
+    rows = out_refs[0].shape[0]
+    for index, out_ref in enumerate(out_refs):
+        part = slice(index * rows, (index + 1) * rows)
+        total = sum(ref[part].astype(F32) for ref in in_refs[-3:]) + in_refs[0][part].astype(F32)
+        out_ref[...] = total.astype(out_ref.dtype)
+
+
+def sum_of(own, arrived, first_type):
+    shape = (own.shape[0] // 4, own.shape[1])
+    vmem = pl.BlockSpec(memory_space=pltpu.VMEM)
+    return pl.pallas_call(
+        sum_kernel,
+        in_specs=[vmem] * 4,
+        out_specs=[vmem] * 4,
+        out_shape=[jax.ShapeDtypeStruct(shape, first_type)] + [jax.ShapeDtypeStruct(shape, BF)] * 3,
+        compiler_params=params(),
+        name="sum",
+    )(own, *arrived)
 
 
 def weight_grad_kernel(offset_ref, cotan_ref, *refs):
@@ -187,13 +226,12 @@
 def attention_kernel(order_ref, q_ref, g_ref, *refs):
     kv_refs, dkv_refs = refs[:4], refs[4:8]
     k_ref, ds0_ref, ds1_ref, v_ref, dk_acc, dv_acc = refs[8:]
-    head = pl.program_id(0)
-    length = q_ref.shape[0]
-    tokens = length // 4
-    mid = length // 2
+    step = pl.program_id(0)
+    length, width = q_ref.shape
+    tokens, mid, heads = length // 4, length // 2, width // HEAD_SIZE
     scale = 1.0 / math.sqrt(HEAD_SIZE)
 
-    @pl.when(head == 0)
+    @pl.when(step == 0)
     def _():
         dk_acc[...] = jnp.zeros_like(dk_acc)
         dv_acc[...] = jnp.zeros_like(dv_acc)
@@ -202,35 +240,64 @@
             k_ref[rows, :] = kv_refs[k][0]
             v_ref[rows, :] = kv_refs[k][1]
 
-    q, g = q_ref[...], g_ref[...]
-    k0, k1 = k_ref[:mid], k_ref[mid:]
-    v0, v1 = v_ref[:mid], v_ref[mid:]
+    early, late = slice(0, mid), slice(mid, length)
     row = lax.broadcasted_iota(jnp.int32, (mid, mid), 0)
     column = lax.broadcasted_iota(jnp.int32, (mid, mid), 1)
     allowed = row <= column
-    e0 = jnp.exp(dot(k0, q, NT) * scale)
-    e0a = jnp.where(allowed, e0[:, :mid], 0.0)
-    e0b = e0[:, mid:]
-    e1 = jnp.where(allowed, jnp.exp(dot(k1, q[mid:], NT) * scale), 0.0)
-    inv_a = 1.0 / jnp.sum(e0a, axis=0, keepdims=True)
-    inv_b = 1.0 / (jnp.sum(e0b, axis=0, keepdims=True) + jnp.sum(e1, axis=0, keepdims=True))
-    p0a, p0b, p1 = e0a * inv_a, e0b * inv_b, e1 * inv_b
-    g_a, g_b = g[:mid], g[mid:]
-    dv_acc[:mid] += dot(p0a.astype(BF), g_a) + dot(p0b.astype(BF), g_b)
-    dv_acc[mid:] += dot(p1.astype(BF), g_b)
-    d0a, d0b, d1 = dot(v0, g_a, NT), dot(v0, g_b, NT), dot(v1, g_b, NT)
-    sum_a = jnp.sum(p0a * d0a, axis=0, keepdims=True)
-    sum_b = jnp.sum(p0b * d0b, axis=0, keepdims=True) + jnp.sum(p1 * d1, axis=0, keepdims=True)
-    s0a = (p0a * (d0a - sum_a)).astype(BF)
-    s0b = (p0b * (d0b - sum_b)).astype(BF)
-    s1 = (p1 * (d1 - sum_b)).astype(BF)
-    ds0_ref[0, :, :mid] = s0a
-    ds0_ref[0, :, mid:] = s0b
-    ds1_ref[0] = s1
-    dk_acc[:mid] += dot(s0a, q[:mid]) + dot(s0b, q[mid:])
-    dk_acc[mid:] += dot(s1, q[mid:])
-
-    @pl.when(head == pl.num_programs(0) - 1)
+    factor = scale * math.log2(math.e)
+    each = range(heads)
+
+    def at(ref, rows, h):
+        return ref[rows, h * HEAD_SIZE : (h + 1) * HEAD_SIZE]
+
+    def products(left_ref, right_ref):
+        return [
+            [
+                dot(left_ref[early], at(right_ref, early, h), NT),
+                dot(left_ref[early], at(right_ref, late, h), NT),
+                dot(left_ref[late], at(right_ref, late, h), NT),
+            ]
+            for h in each
+        ]
+
+    def add(acc, terms, right_ref):
+        acc[early] += sum(
+            dot(terms[h][0], at(right_ref, early, h)) + dot(terms[h][1], at(right_ref, late, h))
+            for h in each
+        )
+        acc[late] += sum(dot(terms[h][2], at(right_ref, late, h)) for h in each)
+
+    def column_sums(terms):
+        first, second, third = (jnp.sum(term, axis=0, keepdims=True) for term in terms)
+        return first, second + third
+
+    scores = products(k_ref, q_ref)
+    d_probs = products(v_ref, g_ref)
+    probs = []
+    for h in each:
+        a, b, c = scores[h]
+        a = jnp.where(allowed, jnp.exp2(a * factor), 0.0)
+        b = jnp.exp2(b * factor)
+        c = jnp.where(allowed, jnp.exp2(c * factor), 0.0)
+        sum_a, sum_b = column_sums((a, b, c))
+        inv_a, inv_b = 1.0 / sum_a, 1.0 / sum_b
+        probs.append((a * inv_a, b * inv_b, c * inv_b))
+    add(dv_acc, [[term.astype(BF) for term in probs[h]] for h in each], g_ref)
+    d_scores = []
+    for h in each:
+        sum_a, sum_b = column_sums([p * d for p, d in zip(probs[h], d_probs[h])])
+        d_scores.append(
+            [
+                (p * (d - total)).astype(BF)
+                for p, d, total in zip(probs[h], d_probs[h], (sum_a, sum_b, sum_b))
+            ]
+        )
+        ds0_ref[h, :, :mid] = d_scores[h][0]
+        ds0_ref[h, :, mid:] = d_scores[h][1]
+        ds1_ref[h] = d_scores[h][2]
+    add(dk_acc, d_scores, q_ref)
+
+    @pl.when(step == pl.num_programs(0) - 1)
     def _():
         for k in range(4):
             rows = pl.ds(pl.multiple_of(order_ref[k] * tokens, tokens), tokens)
@@ -240,19 +307,19 @@
 
 def attention(order, rotated, incoming, pieces):
     length, width = rotated.shape
-    heads, mid = width // HEAD_SIZE, length // 2
-    column = pl.BlockSpec((length, HEAD_SIZE), lambda h: (0, h))
+    heads, mid, pair = width // HEAD_SIZE, length // 2, 2
+    columns = pl.BlockSpec((length, pair * HEAD_SIZE), lambda h: (0, h))
     whole = pl.BlockSpec((length, HEAD_SIZE), lambda h: (0, 0))
     piece = pl.BlockSpec(pieces[0].shape, lambda h: (0, 0, 0))
     result = pl.pallas_call(
         attention_kernel,
-        grid=(heads,),
-        in_specs=[pl.BlockSpec(memory_space=pltpu.SMEM), column, column] + [piece] * 4,
+        grid=(heads // pair,),
+        in_specs=[pl.BlockSpec(memory_space=pltpu.SMEM), columns, columns] + [piece] * 4,
         out_specs=[piece] * 4
         + [
             whole,
-            pl.BlockSpec((1, mid, length), lambda h: (h, 0, 0)),
-            pl.BlockSpec((1, mid, mid), lambda h: (h, 0, 0)),
+            pl.BlockSpec((pair, mid, length), lambda h: (h, 0, 0)),
+            pl.BlockSpec((pair, mid, mid), lambda h: (h, 0, 0)),
         ],
         out_shape=[jax.ShapeDtypeStruct(pieces[0].shape, BF)] * 4
         + [
@@ -262,13 +329,14 @@
         ],
         scratch_shapes=[pltpu.VMEM((length, HEAD_SIZE), BF)]
         + [pltpu.VMEM((length, HEAD_SIZE), F32)] * 2,
-        compiler_params=params(60),
+        compiler_params=params(32),
         name="attention",
     )(order, rotated, incoming, *pieces)
     return result[:4], result[4], result[5], result[6]
 
 
-def grad_query_kernel(q_ref, k_ref, ds0_ref, ds1_ref, cos_ref, sin_ref, out_ref):
+def grad_query_kernel(q_ref, k_ref, ds0_ref, ds1_ref, cos_ref, sin_ref, *refs):
+    out_ref = refs[-1]
     mid = ds0_ref.shape[1]
     scale = 1.0 / math.sqrt(HEAD_SIZE)
     k0, k1 = k_ref[:mid], k_ref[mid:]
@@ -281,27 +349,33 @@
     out_ref[...] = norm_back(field, norm_scale(field), cotan).astype(BF)
 
 
-def grad_queries(queries, key, ds0, ds1, cosines, sines):
+def grad_queries(queries, key, ds0, ds1, cosines, sines, first, given=None):
     length, width = queries.shape
     heads, mid = width // HEAD_SIZE, length // 2
-    column = pl.BlockSpec((length, HEAD_SIZE), lambda h: (0, h))
+    column = pl.BlockSpec((length, HEAD_SIZE), lambda h: (0, first + h))
     whole = pl.BlockSpec((length, HEAD_SIZE), lambda h: (0, 0))
+    specs = [
+        column,
+        whole,
+        pl.BlockSpec((1, mid, length), lambda h: (first + h, 0, 0)),
+        pl.BlockSpec((1, mid, mid), lambda h: (first + h, 0, 0)),
+        whole,
+        whole,
+    ]
+    operands = [queries, key, ds0, ds1, cosines, sines]
+    if given is not None:
+        specs.append(pl.BlockSpec(memory_space=pl.ANY))
+        operands.append(given)
     return pl.pallas_call(
         grad_query_kernel,
-        grid=(heads,),
-        in_specs=[
-            column,
-            whole,
-            pl.BlockSpec((1, mid, length), lambda h: (h, 0, 0)),
-            pl.BlockSpec((1, mid, mid), lambda h: (h, 0, 0)),
-            whole,
-            whole,
-        ],
+        grid=(heads // 2,),
+        in_specs=specs,
         out_specs=column,
         out_shape=jax.ShapeDtypeStruct(queries.shape, BF),
-        compiler_params=params(60),
+        input_output_aliases={} if given is None else {6: 0},
+        compiler_params=params(16),
         name="grad_query",
-    )(queries, key, ds0, ds1, cosines, sines)
+    )(*operands)
 
 
 def cotan_kernel(order_ref, b0_ref, b1_ref, b2_ref, b3_ref, plain_ref, cos_ref, sin_ref, out_ref):
@@ -326,19 +400,19 @@
     )(order, *back, plain, cosines, sines)
 
 
-def grad_token_kernel(x_ref, kept_ref, core_ref, layer_ref, *refs):
+def grad_token_kernel(x_ref, mine_ref, layer_ref, *refs):
     out_ref = refs[-1]
-    cotan = kept_ref[...] + core_ref[...].astype(F32) + layer_ref[...].astype(F32)
+    cotan = mine_ref[...].astype(F32) + layer_ref[...].astype(F32)
     field = x_ref[...].astype(F32)
     out_ref[...] = norm_back(field, norm_scale(field), cotan).astype(BF)
 
 
-def grad_tokens(tokens, kept, from_core, from_layer, start, given=None):
+def grad_tokens(tokens, mine, from_layer, start, given=None):
     step, width = 16, tokens.shape[1]
     first = start // step
     here = pl.BlockSpec((step, width), lambda i: (first + i, 0))
-    specs = [here, here, here, pl.BlockSpec((step, width), lambda i: (i, 0))]
-    operands = [tokens, kept, from_core, from_layer]
+    specs = [here, here, pl.BlockSpec((step, width), lambda i: (i, 0))]
+    operands = [tokens, mine, from_layer]
     if given is not None:
         specs.append(pl.BlockSpec(memory_space=pl.ANY))
         operands.append(given)
@@ -348,8 +422,8 @@
         in_specs=specs,
         out_specs=here,
         out_shape=jax.ShapeDtypeStruct(tokens.shape, BF),
-        input_output_aliases={} if given is None else {4: 0},
-        compiler_params=params(),
+        input_output_aliases={} if given is None else {3: 0},
+        compiler_params=params(60),
         name="grad_tokens",
     )(*operands)
 
@@ -423,14 +497,13 @@
 
     own_weight = key_value_master_weight.astype(BF)
     own_weight = jnp.concatenate([own_weight[0], own_weight[1]], axis=1)
-    stage = jnp.concatenate([to_heads(own_weight, k) for k in range(4)], axis=0)
+    stage_parts = [to_heads(own_weight, k) for k in range(4)]
+    stage = jnp.concatenate(stage_parts, axis=0)
     own_block = normed(tokens)
-    from_core = swap_cores(own_block)
-    from_z = swap_layers(after(stage, own_block)[0])
+    from_z = swap_layers(after(stage_parts[0], own_block)[0])
+    from_core = swap_cores(after(stage, own_block)[0])
     shard = jnp.concatenate([stage, near(stage, 1), near(stage, -1), near(stage, 2)], axis=0)
     pieces = [shard, far(shard, 1), far(shard, -1), far(shard, 2)]
-    (from_z,) = after(pieces, from_z)
-    blocks = [own_block, from_core, from_z, swap_cores(from_z)]
 
     place = jnp.array(PLACES, jnp.int32)
     count = jnp.arange(4, dtype=jnp.int32)
@@ -455,13 +528,19 @@
     own_sin = lax.dynamic_slice_in_dim(sines, t_index * own_tokens, own_tokens, 0)
     rotated = rotated_queries(queries, cosines, sines)
 
-    weights, plain, projected = project(
-        offsets, sequence_order, blocks, own_cos, own_sin,
-        pieces, unit_scale,
+    from_core, from_z, own_cos, own_sin, sequence_order, block_order, offsets = after(
+        (pieces, rotated), from_core, from_z, own_cos, own_sin, sequence_order, block_order, offsets
+    )
+    blocks = [own_block, from_core, from_z, swap_cores(from_z)]
+    weights, plain_early = project_early(offsets, blocks[0], blocks[1], pieces, unit_scale)
+    plain, projected = project(
+        sequence_order, blocks[2], blocks[3], weights, plain_early, own_cos, own_sin, unit_scale
     )
     arrived = [from_heads(block, k) for k, block in enumerate(projected)]
     returning, key, ds0, ds1 = attention(block_order, rotated, grad_out, arrived)
     back = [to_heads(block, -k) for k, block in enumerate(returning)]
+    grad_q = grad_queries(queries, key, ds0, ds1, cosines, sines, 0)
+    (back,) = after(grad_q, back)
     cotan = key_value_cotan(sequence_order, back, plain, own_cos, own_sin)
 
     part = weight_grads(offsets, blocks, cotan)
@@ -474,32 +553,29 @@
     (kept_from,) = after(sent, jnp.concatenate([rows_of[0], rows_of[2]], axis=0))
     kept = dot(kept_from, weights, NT) * unit_scale
     to_z = (kept[own_tokens:] + swapped[own_tokens:].astype(F32)).astype(BF)
-    cuts = (0, 16, 64, own_tokens)
+    cuts = (0, 32, 80, own_tokens)
     to_z = [to_z[cuts[i] : cuts[i + 1]] for i in range(3)]
     z_first = swap_layers(to_z[0])
 
-    own = part[0].astype(F32)
-    for piece in arriving:
-        own = own + piece.astype(F32)
-    own = own.astype(BF).reshape(4, 4 * rows, -1)
-    own, to_z[1] = after(z_first, own, to_z[1])
+    kept, swapped = after(to_z, kept, swapped)
+    mine = (kept[:own_tokens] + swapped[:own_tokens].astype(F32)).astype(BF)
+    grad_x = grad_tokens(tokens, mine, z_first, 0)
+    own_part, to_z[1], mine = after(grad_x, part[0], to_z[1], mine)
+    own = sum_of(own_part, arriving, F32)
     z_second = swap_layers(to_z[1])
-    summed = own[0].astype(F32)
-    for index, step in ((1, -1), (2, 1), (3, 2)):
-        summed = summed + near(own[index], step).astype(F32)
-
-    (ds0,) = after(own, ds0)
-    grad_q = grad_queries(queries, key, ds0, ds1, cosines, sines)
-    (summed,) = after((grad_q, z_second), summed)
-
-    summed = summed.astype(BF).reshape(4, rows, 2 * HEAD_SIZE)
-    final = sum(from_heads(summed[k], -k).astype(F32) for k in range(4)) * unit_scale
+    summed = sum_of(own[0], [near(own[1], -1), near(own[2], 1), near(own[3], 2)], BF)
+    grad_q = grad_queries(
+        queries, key, after(own, ds0)[0], ds1, cosines, sines, queries.shape[1] // HEAD_SIZE // 2, grad_q
+    )
+    (summed,) = after((z_second, grad_q), summed)
+    final = [from_heads(summed[k], -k) for k in range(4)]
+    grad_x = grad_tokens(tokens, mine, after(summed, z_second)[0], cuts[1], grad_x)
+    (final,) = after(grad_x, final)
+    final = sum(block.astype(F32) for block in final) * unit_scale
     weight_grad = jnp.stack([final[:, :HEAD_SIZE], final[:, HEAD_SIZE:]], axis=0)
 
-    z_first, z_second, to_z[2] = after(final, z_first, z_second, to_z[2])
-    grad_x = grad_tokens(tokens, kept, swapped, z_first, 0)
-    grad_x = grad_tokens(tokens, kept, swapped, z_second, cuts[1], grad_x)
-    grad_x = grad_tokens(tokens, kept, swapped, swap_layers(to_z[2]), cuts[2], grad_x)
+    (to_z[2],) = after(final, to_z[2])
+    grad_x = grad_tokens(tokens, mine, swap_layers(to_z[2]), cuts[2], grad_x)
 
     new_first = beta_one * key_value_first_moment + (1.0 - beta_one) * weight_grad
     new_second = beta_two * key_value_second_moment + (1.0 - beta_two) * weight_grad * weight_grad
@@ -509,10 +585,12 @@
         first_hat / (jnp.sqrt(second_hat) + adam_eps) + weight_decay * key_value_master_weight
     )
     replicas = writer.shape[0]
-    flat_saved = new_master.astype(BF).reshape(replicas, -1)
+    pieces = new_master.astype(BF).reshape(replicas, 2, -1)
     rank_ids = jnp.arange(replicas, dtype=jnp.int32)
     inverse = jnp.sum(jnp.where(writer[None, :] == rank_ids[:, None], rank_ids[None, :], 0), axis=1)
-    saved = lax.all_to_all(flat_saved[inverse], ("zl", "x", "y", "c"), 0, 0, tiled=True)
+    outgoing = pieces.at[inverse].get(mode="promise_in_bounds")
+    saved = lax.all_to_all(outgoing, ("zl", "x", "y", "c"), 0, 0, tiled=True)
+    saved = after(grad_x, saved)[0].reshape(replicas, -1)
     return (grad_x, grad_q, new_master, new_first, new_second, saved)
 
 

time: 187 us -> 172 us (0.920)
  starting transfers between devices: 85.5 us -> 79.6 us
  Pallas kernels: 41.8 us -> 38.3 us
  waiting for transfers between devices: 35.4 us -> 32.6 us
  local copies, waits for them, and re-layouts: 14.1 us -> 12.2 us
    ppermute x4, waiting for transfers between devices: 2.16 us -> 10.7 us  [swap_layers(): return lax.ppermute(block, 'zl', [(0, 1), (1, 0)])]
    ppermute x3, starting transfers between devices: 12.7 us -> 4.45 us  [swap_cores(): return lax.ppermute(block, 'c', [(0, 1), (1, 0)])]
    ppermute x6, waiting for transfers between devices: 17.2 us -> 12.1 us  [far(): return lax.ppermute(block, ('x', 'y', 'c'), plane_pairs(True, step))]
    pallas_call x3 -> x7, Pallas kernels: 24.9 us -> 20.1 us  [the longest x2 6.45 us: grad_queries(): pl.pallas_call(grad_query_kernel, grid=(heads // 2,), in_specs=specs, out...]
    ppermute x8, waiting for transfers between devices: 6.78 us -> 2.95 us  [from_heads(): lax.ppermute(block, ('zl', 'c', 't'), group_pairs(lambda g, t: (t + k, g)))]
    ppermute x8, starting transfers between devices: 17.6 us -> 21.4 us  [from_heads(): lax.ppermute(block, ('zl', 'c', 't'), group_pairs(lambda g, t: (t + k, g)))]
    ppermute x8, waiting for transfers between devices: 3.39 us -> 0.02 us  [to_heads(): lax.ppermute(block, ('zl', 'c', 't'), group_pairs(lambda g, t: (t, g + k)))]
    ppermute x4, starting transfers between devices: 8.54 us -> 6.41 us  [swap_layers(): return lax.ppermute(block, 'zl', [(0, 1), (1, 0)])]
  transfers between devices with their start and end apart: 36 -> 36, of which waited for: 14 -> 15; matrix products, arithmetic and copies ran while one was open for 7% -> 6% of each run, Pallas kernels for 9% -> 14%
where the time goes in v1:
time: 172 us; the launch traced here: 171 us
  starting transfers between devices  79.6 us (46%)
  Pallas kernels  38.3 us (22%)
  waiting for transfers between devices  32.6 us (19%)
  local copies, waits for them, and re-layouts  12.2 us (7%)
  other arithmetic  5.5 us (3%)
  matrix products  1.76 us (1%)
    ppermute x8, starting transfers between devices, to_heads(): lax.ppermute(block, ('zl', 'c', 't'), group_pairs(lambda g, t: (t, g + k)))  24.6 us
    ppermute x8, starting transfers between devices, from_heads(): lax.ppermute(block, ('zl', 'c', 't'), group_pairs(lambda g, t: (t + k, g)))  21.4 us
    ppermute x6, waiting for transfers between devices, far(): return lax.ppermute(block, ('x', 'y', 'c'), plane_pairs(True, step))  12.1 us
    ppermute x4, waiting for transfers between devices, swap_layers(): return lax.ppermute(block, 'zl', [(0, 1), (1, 0)])  10.7 us
    pallas_call x3, Pallas kernels, grad_tokens(): pl.pallas_call(grad_token_kernel, grid=(from_layer.shape[0] // step,), in...  8.96 us
    ppermute x6, starting transfers between devices, near(): return lax.ppermute(block, ('x', 'y', 'c'), plane_pairs(False, step))  8.88 us
    unnamed x37, local copies, waits for them, and re-layouts  8.22 us
    ppermute x6, starting transfers between devices, far(): return lax.ppermute(block, ('x', 'y', 'c'), plane_pairs(True, step))  8.15 us
  transfers between devices with their start and end apart: 36, of which 15 were waited for; matrix products, arithmetic and copies ran while one was open for 6% of the time, Pallas kernels for 14%

profile of v1, /device:TPU:1, one launch (start us, length us, event | category | flops | bytes accessed | tf_op | source)
XLA Modules:
  0.0 171.0 jit_solution(2943862880646751617)
XLA Ops:
  1.5 6.3 %collective-permute-start = (bf16[80,256]{1,0:T(8,128)(2,1)S(1)}, bf16[80,256]{1,0:T(8,128)(2,1)S(1)}, u32[]{:S(2)}, u32[]{:S(2)}) collective-permute-start(bf16[80,256]{1,0:T(8,128)(2,1)S(1)} %pad_maximum_fusion.4), channel_id=1, source_target_pairs={{0,0},{1,4},{2,128},{3,132},{4,1},{5,5},{6,129},{7,133},{128,2},{1... | collective-permute-start | bytes 122888 | tf_op jit(solution)/shard_map/ppermute | solution.py:465
  7.8 4.0 %collective-permute-start.1 = (bf16[80,256]{1,0:T(8,128)(2,1)S(1)}, bf16[80,256]{1,0:T(8,128)(2,1)S(1)}, u32[]{:S(2)}, u32[]{:S(2)}) collective-permute-start(bf16[80,256]{1,0:T(8,128)(2,1)S(1)} %pad_maximum_fusion.4), channel_id=1, source_target_pairs={{0,1},{1,5},{2,129},{3,133},{4,2},{5,6},{6,130},{7,134},{128,3},{1... | collective-permute-start | bytes 122888 | tf_op jit(solution)/shard_map/ppermute | solution.py:465
  11.9 3.3 %collective-permute-start.2 = (bf16[80,256]{1,0:T(8,128)(2,1)S(1)}, bf16[80,256]{1,0:T(8,128)(2,1)S(1)}, u32[]{:S(2)}, u32[]{:S(2)}) collective-permute-start(bf16[80,256]{1,0:T(8,128)(2,1)S(1)} %pad_maximum_fusion.4), channel_id=1, source_target_pairs={{0,2},{1,6},{2,130},{3,134},{4,3},{5,7},{6,131},{7,135},{128,0},{1... | collective-permute-start | bytes 122888 | tf_op jit(solution)/shard_map/ppermute | solution.py:465
  29.2 3.1 %collective-permute-done.6 = bf16[320,256]{1,0:T(8,128)(2,1)S(1)} collective-permute-done((bf16[320,256]{1,0:T(8,128)(2,1)}, bf16[320,256]{1,0:T(8,128)(2,1)S(1)}, u32[]{:S(2)}, u32[]{:S(2)}) %collective-permute-start.6) | collective-permute-done | bytes 163872 | tf_op jit(solution)/shard_map/ppermute | solution.py:448
  40.2 3.2 %collective-permute-done.7.refs_1_ = bf16[1280,256]{1,0:T(8,128)(2,1)S(1)} collective-permute-done((bf16[1280,256]{1,0:T(8,128)(2,1)S(1)}, bf16[1280,256]{1,0:T(8,128)(2,1)S(1)}, u32[]{:S(2)}, u32[]{:S(2)}) %collective-permute-start.7) | collective-permute-done | bytes 655392 | tf_op jit(solution)/shard_map/ppermute | solution.py:444
  43.4 6.4 %collective-permute-done.8.refs_2_ = bf16[1280,256]{1,0:T(8,128)(2,1)S(1)} collective-permute-done((bf16[1280,256]{1,0:T(8,128)(2,1)S(1)}, bf16[1280,256]{1,0:T(8,128)(2,1)S(1)}, u32[]{:S(2)}, u32[]{:S(2)}) %collective-permute-start.8) | collective-permute-done | bytes 655392 | tf_op jit(solution)/shard_map/ppermute | solution.py:444
  54.1 3.6 %project_early.1 = (bf16[5120,256]{1,0:T(8,128)(2,1)}, f32[256,256]{1,0:T(8,128)S(1)}) custom-call(s32[64]{0:T(128)S(1)} %add.170.offset_ref, bf16[128,5120]{1,0:T(8,128)(2,1)S(1)} %norm.1.first_ref.refs_0_, bf16[128,5120]{1,0:T(8,128)(2,1)} %collective-permute-done.10.second_ref.refs_1_, bf16[1280,256]{1,0:T(8,128)(2,1)S(1)} %constant_dynamic-update-slice_fusion.4.refs_0_, ...), custom_call_target="tpu_custom_call" | custom-call | tf_op jit(solution)/shard_map/project_early/pallas_call | solution.py:129
  65.9 5.8 %collective-permute-start.16 = (bf16[2,128,128]{2,1,0:T(8,128)(2,1)S(1)}, bf16[2,128,128]{2,1,0:T(8,128)(2,1)S(1)}, u32[]{:S(2)}, u32[]{:S(2)}) collective-permute-start(bf16[2,128,128]{2,1,0:T(8,128)(2,1)S(1)} %get-tuple-element.78), channel_id=1, source_target_pairs={{0,132},{1,0},{2,4},{3,128},{4,133},{5,1},{6,5},{7,129},{128,134},... | collective-permute-start | bytes 196616 | tf_op jit(solution)/shard_map/ppermute | solution.py:469
  74.2 5.9 %attention.1 = (bf16[2,128,128]{2,1,0:T(8,128)(2,1)S(1)}, bf16[2,128,128]{2,1,0:T(8,128)(2,1)S(1)}, bf16[2,128,128]{2,1,0:T(8,128)(2,1)S(1)}, bf16[2,128,128]{2,...) custom-call(s32[4]{0:T(128)S(1)} %get-tuple-element.68.order_ref, ...), custom_call_target="tpu_custom_call" | custom-call | tf_op jit(solution)/shard_map/attention/pallas_call | solution.py:314
  80.0 2.9 %collective-permute-start.17 = (bf16[2,128,128]{2,1,0:T(8,128)(2,1)S(1)}, bf16[2,128,128]{2,1,0:T(8,128)(2,1)S(1)}, u32[]{:S(2)}, u32[]{:S(2)}) collective-permute-start(bf16[2,128,128]{2,1,0:T(8,128)(2,1)S(1)} %get-tuple-element.82), channel_id=1, source_target_pairs={{0,0},{1,4},{2,128},{3,132},{4,1},{5,5},{6,129},{7,133},{128,2},{1... | collective-permute-start | bytes 196616 | tf_op jit(solution)/shard_map/ppermute | solution.py:465
  83.0 4.2 %collective-permute-start.19 = (bf16[2,128,128]{2,1,0:T(8,128)(2,1)S(1)}, bf16[2,128,128]{2,1,0:T(8,128)(2,1)S(1)}, u32[]{:S(2)}, u32[]{:S(2)}) collective-permute-start(bf16[2,128,128]{2,1,0:T(8,128)(2,1)S(1)} %get-tuple-element.84), channel_id=1, source_target_pairs={{0,2},{1,6},{2,130},{3,134},{4,3},{5,7},{6,131},{7,135},{128,0},{1... | collective-permute-start | bytes 196616 | tf_op jit(solution)/shard_map/ppermute | solution.py:465
  87.2 3.9 %collective-permute-start.20 = (bf16[2,128,128]{2,1,0:T(8,128)(2,1)S(1)}, bf16[2,128,128]{2,1,0:T(8,128)(2,1)S(1)}, u32[]{:S(2)}, u32[]{:S(2)}) collective-permute-start(bf16[2,128,128]{2,1,0:T(8,128)(2,1)S(1)} %get-tuple-element.85), channel_id=1, source_target_pairs={{0,1},{1,5},{2,129},{3,133},{4,2},{5,6},{6,130},{7,134},{128,3},{1... | collective-permute-start | bytes 196616 | tf_op jit(solution)/shard_map/ppermute | solution.py:465
  91.1 3.2 %grad_query.2.refs_0_ = bf16[512,1024]{1,0:T(8,128)(2,1)} custom-call(bf16[512,1024]{1,0:T(8,128)(2,1)S(1)} %copy-done.3, bf16[512,128]{1,0:T(8,128)(2,1)S(1)} %get-tuple-element.79.k_ref, bf16[8,256,512]{2,1,0:T(8,128)(2,1)S(1)} %get-tuple-element.106.ds0_ref, bf16[8,256,256]{2,1,0:T(8,128)(2,1)S(1)} %get-tuple-element.81.ds1_ref, ...), custom_call_target="tpu_custom_call" | custom-call | tf_op jit(solution)/shard_map/grad_query/pallas_call | solution.py:369
  95.3 5.3 %weight_grads.1 = (bf16[1280,256]{1,0:T(8,128)(2,1)S(1)}, bf16[1280,256]{1,0:T(8,128)(2,1)}, bf16[1280,256]{1,0:T(8,128)(2,1)}, bf16[1280,256]{1,0:T(8,128)(2,1)}) custom-call(s32[64]{0:T(128)S(1)} %add.170.offset_ref, bf16[512,256]{1,0:T(8,128)(2,1)S(1)} %key_value_cotan.1.cotan_ref, bf16[128,5120]{1,0:T(8,128)(2,1)S(1)} %norm.1.first_ref.refs_0_, ...), custom_call_target="tpu_custom_call" | custom-call | tf_op jit(solution)/shard_map/weight_grads/pallas_call | solution.py:215
  109.9 2.7 %collective-permute-start.22 = (bf16[32,5120]{1,0:T(8,128)(2,1)S(1)}, bf16[32,5120]{1,0:T(8,128)(2,1)}, u32[]{:S(2)}, u32[]{:S(2)}) collective-permute-start(bf16[32,5120]{1,0:T(8,128)(2,1)S(1)} %slice.70), channel_id=1, source_target_pairs={{0,128},{128,0},{1,129},{129,1},{2,130},{130,2},{3,131},{131,3},{4... | collective-permute-start | bytes 983048 | tf_op jit(solution)/shard_map/ppermute | solution.py:473
  113.9 6.2 %collective-permute-done.22.layer_ref = bf16[32,5120]{1,0:T(8,128)(2,1)} collective-permute-done((bf16[32,5120]{1,0:T(8,128)(2,1)S(1)}, bf16[32,5120]{1,0:T(8,128)(2,1)}, u32[]{:S(2)}, u32[]{:S(2)}) %collective-permute-start.22) | collective-permute-done | bytes 327712 | tf_op jit(solution)/shard_map/ppermute | solution.py:473
  125.9 2.8 %collective-permute-start.27 = (bf16[320,256]{1,0:T(8,128)(2,1)S(1)}, bf16[320,256]{1,0:T(8,128)(2,1)S(1)}, u32[]{:S(2)}, u32[]{:S(2)}) collective-permute-start(bf16[320,256]{1,0:T(8,128)(2,1)S(1)} %get-tuple-element.103), channel_id=1, source_target_pairs={{0,24},{4,100},{8,0},{12,108},{16,8},{20,116},{24,16},{28,124},{32... | collective-permute-start | bytes 491528 | tf_op jit(solution)/shard_map/ppermute | solution.py:448
  132.1 3.2 %grad_query.3 = bf16[512,1024]{1,0:T(8,128)(2,1)} custom-call(bf16[512,1024]{1,0:T(8,128)(2,1)S(1)} %copy-done.3, bf16[512,128]{1,0:T(8,128)(2,1)S(1)} %get-tuple-element.79.k_ref, bf16[8,256,512]{2,1,0:T(8,128)(2,1)S(1)} %copy-done.5, bf16[8,256,256]{2,1,0:T(8,128)(2,1)S(1)} %get-tuple-element.81.ds1_ref, ...), custom_call_target="tpu_custom_call", output_to_operand_aliasing={{}: (6, {})} | custom-call | tf_op jit(solution)/shard_map/grad_query/pallas_call | solution.py:369
  136.2 6.9 %collective-permute-start.30 = (bf16[80,256]{1,0:T(8,128)(2,1)S(1)}, bf16[80,256]{1,0:T(8,128)(2,1)S(1)}, u32[]{:S(2)}, u32[]{:S(2)}) collective-permute-start(bf16[80,256]{1,0:T(8,128)(2,1)S(1)} %get-tuple-element.111), channel_id=1, source_target_pairs={{0,0},{1,4},{2,128},{3,132},{4,1},{5,5},{6,129},{7,133},{128,2},{1... | collective-permute-start | bytes 122888 | tf_op jit(solution)/shard_map/ppermute | solution.py:469
  144.2 3.7 %collective-permute-start.32 = (bf16[80,256]{1,0:T(8,128)(2,1)S(1)}, bf16[80,256]{1,0:T(8,128)(2,1)S(1)}, u32[]{:S(2)}, u32[]{:S(2)}) collective-permute-start(bf16[80,256]{1,0:T(8,128)(2,1)S(1)} %get-tuple-element.113), channel_id=1, source_target_pairs={{0,128},{1,132},{2,0},{3,4},{4,129},{5,133},{6,1},{7,5},{128,130},... | collective-permute-start | bytes 122888 | tf_op jit(solution)/shard_map/ppermute | solution.py:469
  147.9 3.4 %grad_tokens.4.refs_0_ = bf16[128,5120]{1,0:T(8,128)(2,1)} custom-call(bf16[128,5120]{1,0:T(8,128)(2,1)} %x_ref.5, bf16[128,5120]{1,0:T(8,128)(2,1)} %add_convert_fusion.mine_ref, bf16[48,5120]{1,0:T(8,128)(2,1)} %copy-done.10, bf16[128,5120]{1,0:T(8,128)(2,1)} %grad_tokens.3.refs_0_), custom_call_target="tpu_custom_call", output_to_operand_aliasing={{}: (3, {})} | custom-call | tf_op jit(solution)/shard_map/grad_tokens/pallas_call | solution.py:419
  156.4 5.6 %all-to-all-start = ((bf16[64,2,160]{2,1,0:T(2,128)(2,1)}), bf16[64,2,160]{2,1,0:T(2,128)(2,1)S(1)}, u32[]{:S(2)}, u32[]{:S(2)}) async-start(bf16[64,2,160]{2,1,0:T(2,128)(2,1)} %gather_fusion), calls=%async_computation | async-start | bytes 131072 | tf_op jit(solution)/shard_map/all_to_all | solution.py:592
  162.1 2.7 %collective-permute-done.34.layer_ref = bf16[48,5120]{1,0:T(8,128)(2,1)S(1)} collective-permute-done((bf16[48,5120]{1,0:T(8,128)(2,1)S(1)}, bf16[48,5120]{1,0:T(8,128)(2,1)S(1)}, u32[]{:S(2)}, u32[]{:S(2)}) %collective-permute-start.34) | collective-permute-done | bytes 491552 | tf_op jit(solution)/shard_map/ppermute | solution.py:473
  165.5 3.4 %grad_tokens.5 = bf16[128,5120]{1,0:T(8,128)(2,1)} custom-call(bf16[128,5120]{1,0:T(8,128)(2,1)} %x_ref.5, bf16[128,5120]{1,0:T(8,128)(2,1)} %add_convert_fusion.mine_ref, bf16[48,5120]{1,0:T(8,128)(2,1)} %copy-done.11, bf16[128,5120]{1,0:T(8,128)(2,1)} %grad_tokens.4.refs_0_), custom_call_target="tpu_custom_call", output_to_operand_aliasing={{}: (3, {})} | custom-call | tf_op jit(solution)/shard_map/grad_tokens/pallas_call | solution.py:419
  (130 shorter events, 68.2 us)
Async XLA Ops:
  1.5 16.4 %collective-permute-start = (bf16[80,256]{1,0:T(8,128)(2,1)S(1)}, bf16[80,256]{1,0:T(8,128)(2,1)S(1)}, u32[]{:S(2)}, u32[]{:S(2)}) collective-permute-start(bf16[80,256]{1,0:T(8,128)(2,1)S(1)} %pad_maximum_fusion.4), channel_id=1, source_target_pairs={{0,0},{1,4},{2,128},{3,132},{4,1},{5,5},{6,129},{7,133},{128,2},{1... | collective-permute-start | bytes 122888 | tf_op jit(solution)/shard_map/ppermute | solution.py:465
  7.8 10.7 %collective-permute-start.1 = (bf16[80,256]{1,0:T(8,128)(2,1)S(1)}, bf16[80,256]{1,0:T(8,128)(2,1)S(1)}, u32[]{:S(2)}, u32[]{:S(2)}) collective-permute-start(bf16[80,256]{1,0:T(8,128)(2,1)S(1)} %pad_maximum_fusion.4), channel_id=1, source_target_pairs={{0,1},{1,5},{2,129},{3,133},{4,2},{5,6},{6,130},{7,134},{128,3},{1... | collective-permute-start | bytes 122888 | tf_op jit(solution)/shard_map/ppermute | solution.py:465
  20.4 31.1 %collective-permute-start.10 = (bf16[128,5120]{1,0:T(8,128)(2,1)S(1)}, bf16[128,5120]{1,0:T(8,128)(2,1)}, u32[]{:S(2)}, u32[]{:S(2)}) collective-permute-start(bf16[128,5120]{1,0:T(8,128)(2,1)S(1)} %norm.1.first_ref.refs_0_), channel_id=1, source_target_pairs={{0,4},{4,0},{1,5},{5,1},{2,6},{6,2},{3,7},{7,3},{8,12},{12,8},{9,1... | collective-permute-start | bytes 3932168 | tf_op jit(solution)/shard_map/ppermute | solution.py:452
  22.8 30.5 %collective-permute-start.11 = (bf16[128,5120]{1,0:T(8,128)(2,1)S(1)}, bf16[128,5120]{1,0:T(8,128)(2,1)}, u32[]{:S(2)}, u32[]{:S(2)}) collective-permute-start(bf16[128,5120]{1,0:T(8,128)(2,1)S(1)} %norm.1.first_ref.refs_0_), channel_id=1, source_target_pairs={{0,128},{128,0},{1,129},{129,1},{2,130},{130,2},{3,131},{131,3},{4... | collective-permute-start | bytes 3932168 | tf_op jit(solution)/shard_map/ppermute | solution.py:473
  32.3 11.1 %collective-permute-start.7 = (bf16[1280,256]{1,0:T(8,128)(2,1)S(1)}, bf16[1280,256]{1,0:T(8,128)(2,1)S(1)}, u32[]{:S(2)}, u32[]{:S(2)}) collective-permute-start(bf16[1280,256]{1,0:T(8,128)(2,1)S(1)} %constant_dynamic-update-slice_fusion.4.refs_0_), channel_id=1, source_target_pairs={{0,32},{4,12},{8,40},{12,20},{16,48},{20,28},{24,56},{28,4},{32,64... | collective-permute-start | bytes 1966088 | tf_op jit(solution)/shard_map/ppermute | solution.py:444
  33.4 16.4 %collective-permute-start.8 = (bf16[1280,256]{1,0:T(8,128)(2,1)S(1)}, bf16[1280,256]{1,0:T(8,128)(2,1)S(1)}, u32[]{:S(2)}, u32[]{:S(2)}) collective-permute-start(bf16[1280,256]{1,0:T(8,128)(2,1)S(1)} %constant_dynamic-update-slice_fusion.4.refs_0_), channel_id=1, source_target_pairs={{0,96},{4,28},{8,104},{12,4},{16,112},{20,12},{24,120},{28,20},{32... | collective-permute-start | bytes 1966088 | tf_op jit(solution)/shard_map/ppermute | solution.py:444
  35.2 16.4 %collective-permute-start.9 = (bf16[1280,256]{1,0:T(8,128)(2,1)S(1)}, bf16[1280,256]{1,0:T(8,128)(2,1)S(1)}, u32[]{:S(2)}, u32[]{:S(2)}) collective-permute-start(bf16[1280,256]{1,0:T(8,128)(2,1)S(1)} %constant_dynamic-update-slice_fusion.4.refs_0_), channel_id=1, source_target_pairs={{0,64},{4,20},{8,72},{12,28},{16,80},{20,4},{24,88},{28,12},{32,96... | collective-permute-start | bytes 1966088 | tf_op jit(solution)/shard_map/ppermute | solution.py:444
  62.0 9.8 %collective-permute-start.13 = (bf16[2,128,128]{2,1,0:T(8,128)(2,1)S(1)}, bf16[2,128,128]{2,1,0:T(8,128)(2,1)S(1)}, u32[]{:S(2)}, u32[]{:S(2)}) collective-permute-start(bf16[2,128,128]{2,1,0:T(8,128)(2,1)S(1)} %get-tuple-element.75), channel_id=1, source_target_pairs={{0,0},{1,4},{2,128},{3,132},{4,1},{5,5},{6,129},{7,133},{128,2},{1... | collective-permute-start | bytes 196616 | tf_op jit(solution)/shard_map/ppermute | solution.py:469
  64.5 8.5 %collective-permute-start.15 = (bf16[2,128,128]{2,1,0:T(8,128)(2,1)S(1)}, bf16[2,128,128]{2,1,0:T(8,128)(2,1)S(1)}, u32[]{:S(2)}, u32[]{:S(2)}) collective-permute-start(bf16[2,128,128]{2,1,0:T(8,128)(2,1)S(1)} %get-tuple-element.77), channel_id=1, source_target_pairs={{0,128},{1,132},{2,0},{3,4},{4,129},{5,133},{6,1},{7,5},{128,130},... | collective-permute-start | bytes 196616 | tf_op jit(solution)/shard_map/ppermute | solution.py:469
  65.9 8.2 %collective-permute-start.16 = (bf16[2,128,128]{2,1,0:T(8,128)(2,1)S(1)}, bf16[2,128,128]{2,1,0:T(8,128)(2,1)S(1)}, u32[]{:S(2)}, u32[]{:S(2)}) collective-permute-start(bf16[2,128,128]{2,1,0:T(8,128)(2,1)S(1)} %get-tuple-element.78), channel_id=1, source_target_pairs={{0,132},{1,0},{2,4},{3,128},{4,133},{5,1},{6,5},{7,129},{128,134},... | collective-permute-start | bytes 196616 | tf_op jit(solution)/shard_map/ppermute | solution.py:469
  80.0 14.3 %collective-permute-start.17 = (bf16[2,128,128]{2,1,0:T(8,128)(2,1)S(1)}, bf16[2,128,128]{2,1,0:T(8,128)(2,1)S(1)}, u32[]{:S(2)}, u32[]{:S(2)}) collective-permute-start(bf16[2,128,128]{2,1,0:T(8,128)(2,1)S(1)} %get-tuple-element.82), channel_id=1, source_target_pairs={{0,0},{1,4},{2,128},{3,132},{4,1},{5,5},{6,129},{7,133},{128,2},{1... | collective-permute-start | bytes 196616 | tf_op jit(solution)/shard_map/ppermute | solution.py:465
  82.9 11.4 %collective-permute-start.18 = (bf16[2,128,128]{2,1,0:T(8,128)(2,1)S(1)}, bf16[2,128,128]{2,1,0:T(8,128)(2,1)S(1)}, u32[]{:S(2)}, u32[]{:S(2)}) collective-permute-start(bf16[2,128,128]{2,1,0:T(8,128)(2,1)S(1)} %get-tuple-element.83), channel_id=1, source_target_pairs={{0,3},{1,7},{2,131},{3,135},{4,0},{5,4},{6,128},{7,132},{128,1},{1... | collective-permute-start | bytes 196616 | tf_op jit(solution)/shard_map/ppermute | solution.py:465
  83.0 11.3 %collective-permute-start.19 = (bf16[2,128,128]{2,1,0:T(8,128)(2,1)S(1)}, bf16[2,128,128]{2,1,0:T(8,128)(2,1)S(1)}, u32[]{:S(2)}, u32[]{:S(2)}) collective-permute-start(bf16[2,128,128]{2,1,0:T(8,128)(2,1)S(1)} %get-tuple-element.84), channel_id=1, source_target_pairs={{0,2},{1,6},{2,130},{3,134},{4,3},{5,7},{6,131},{7,135},{128,0},{1... | collective-permute-start | bytes 196616 | tf_op jit(solution)/shard_map/ppermute | solution.py:465
  103.6 19.9 %collective-permute-start.24 = (bf16[1280,256]{1,0:T(8,128)(2,1)}, bf16[1280,256]{1,0:T(8,128)(2,1)S(1)}, u32[]{:S(2)}, u32[]{:S(2)}) collective-permute-start(bf16[1280,256]{1,0:T(8,128)(2,1)} %get-tuple-element.99), channel_id=1, source_target_pairs={{0,96},{4,28},{8,104},{12,4},{16,112},{20,12},{24,120},{28,20},{32... | collective-permute-start | bytes 1966088 | tf_op jit(solution)/shard_map/ppermute | solution.py:444
  106.0 18.3 %collective-permute-start.25 = (bf16[1280,256]{1,0:T(8,128)(2,1)}, bf16[1280,256]{1,0:T(8,128)(2,1)}, u32[]{:S(2)}, u32[]{:S(2)}) collective-permute-start(bf16[1280,256]{1,0:T(8,128)(2,1)} %get-tuple-element.100), channel_id=1, source_target_pairs={{0,32},{4,12},{8,40},{12,20},{16,48},{20,28},{24,56},{28,4},{32,64... | collective-permute-start | bytes 1966088 | tf_op jit(solution)/shard_map/ppermute | solution.py:444
  106.0 18.3 %collective-permute-start.26 = (bf16[1280,256]{1,0:T(8,128)(2,1)}, bf16[1280,256]{1,0:T(8,128)(2,1)}, u32[]{:S(2)}, u32[]{:S(2)}) collective-permute-start(bf16[1280,256]{1,0:T(8,128)(2,1)} %get-tuple-element.101), channel_id=1, source_target_pairs={{0,64},{4,20},{8,72},{12,28},{16,80},{20,4},{24,88},{28,12},{32,96... | collective-permute-start | bytes 1966088 | tf_op jit(solution)/shard_map/ppermute | solution.py:444
  109.9 10.3 %collective-permute-start.22 = (bf16[32,5120]{1,0:T(8,128)(2,1)S(1)}, bf16[32,5120]{1,0:T(8,128)(2,1)}, u32[]{:S(2)}, u32[]{:S(2)}) collective-permute-start(bf16[32,5120]{1,0:T(8,128)(2,1)S(1)} %slice.70), channel_id=1, source_target_pairs={{0,128},{128,0},{1,129},{129,1},{2,130},{130,2},{3,131},{131,3},{4... | collective-permute-start | bytes 983048 | tf_op jit(solution)/shard_map/ppermute | solution.py:473
  122.3 13.9 %collective-permute-start.23 = (bf16[48,5120]{1,0:T(8,128)(2,1)}, bf16[48,5120]{1,0:T(8,128)(2,1)S(1)}, u32[]{:S(2)}, u32[]{:S(2)}) collective-permute-start(bf16[48,5120]{1,0:T(8,128)(2,1)} %get-tuple-element.97), channel_id=1, source_target_pairs={{0,128},{128,0},{1,129},{129,1},{2,130},{130,2},{3,131},{131,3},{4... | collective-permute-start | bytes 1474568 | tf_op jit(solution)/shard_map/ppermute | solution.py:473
  125.9 9.4 %collective-permute-start.27 = (bf16[320,256]{1,0:T(8,128)(2,1)S(1)}, bf16[320,256]{1,0:T(8,128)(2,1)S(1)}, u32[]{:S(2)}, u32[]{:S(2)}) collective-permute-start(bf16[320,256]{1,0:T(8,128)(2,1)S(1)} %get-tuple-element.103), channel_id=1, source_target_pairs={{0,24},{4,100},{8,0},{12,108},{16,8},{20,116},{24,16},{28,124},{32... | collective-permute-start | bytes 491528 | tf_op jit(solution)/shard_map/ppermute | solution.py:448
  136.2 15.1 %collective-permute-start.30 = (bf16[80,256]{1,0:T(8,128)(2,1)S(1)}, bf16[80,256]{1,0:T(8,128)(2,1)S(1)}, u32[]{:S(2)}, u32[]{:S(2)}) collective-permute-start(bf16[80,256]{1,0:T(8,128)(2,1)S(1)} %get-tuple-element.111), channel_id=1, source_target_pairs={{0,0},{1,4},{2,128},{3,132},{4,1},{5,5},{6,129},{7,133},{128,2},{1... | collective-permute-start | bytes 122888 | tf_op jit(solution)/shard_map/ppermute | solution.py:469
  143.2 8.2 %collective-permute-start.31 = (bf16[80,256]{1,0:T(8,128)(2,1)S(1)}, bf16[80,256]{1,0:T(8,128)(2,1)S(1)}, u32[]{:S(2)}, u32[]{:S(2)}) collective-permute-start(bf16[80,256]{1,0:T(8,128)(2,1)S(1)} %get-tuple-element.112), channel_id=1, source_target_pairs={{0,132},{1,0},{2,4},{3,128},{4,133},{5,1},{6,5},{7,129},{128,134},... | collective-permute-start | bytes 122888 | tf_op jit(solution)/shard_map/ppermute | solution.py:469
  144.2 7.7 %collective-permute-start.32 = (bf16[80,256]{1,0:T(8,128)(2,1)S(1)}, bf16[80,256]{1,0:T(8,128)(2,1)S(1)}, u32[]{:S(2)}, u32[]{:S(2)}) collective-permute-start(bf16[80,256]{1,0:T(8,128)(2,1)S(1)} %get-tuple-element.113), channel_id=1, source_target_pairs={{0,128},{1,132},{2,0},{3,4},{4,129},{5,133},{6,1},{7,5},{128,130},... | collective-permute-start | bytes 122888 | tf_op jit(solution)/shard_map/ppermute | solution.py:469
  151.9 12.8 %collective-permute-start.34 = (bf16[48,5120]{1,0:T(8,128)(2,1)S(1)}, bf16[48,5120]{1,0:T(8,128)(2,1)S(1)}, u32[]{:S(2)}, u32[]{:S(2)}) collective-permute-start(bf16[48,5120]{1,0:T(8,128)(2,1)S(1)} %copy-done.9), channel_id=1, source_target_pairs={{0,128},{128,0},{1,129},{129,1},{2,130},{130,2},{3,131},{131,3},{4... | collective-permute-start | bytes 1474568 | tf_op jit(solution)/shard_map/ppermute | solution.py:473
  156.4 13.8 %all-to-all-start = ((bf16[64,2,160]{2,1,0:T(2,128)(2,1)}), bf16[64,2,160]{2,1,0:T(2,128)(2,1)S(1)}, u32[]{:S(2)}, u32[]{:S(2)}) async-start(bf16[64,2,160]{2,1,0:T(2,128)(2,1)} %gather_fusion), calls=%async_computation | async-start | bytes 131072 | tf_op jit(solution)/shard_map/all_to_all | solution.py:592
  (28 other events, 189.6 us)
